TPU v7x, 32 devices: a whole 2x2x4 slice. The times are simulated.
32 devices in a mesh: fsdp: 16 (over z, y, x), dp: 2 (over core).
Axes of the slice: x: 2, y: 2, z: 4, core: 2. Of those that a mesh axis runs over, the one named last changes fastest.
Arguments:
- clips_wide: bfloat16 [32, 102, 768], P(('fsdp', 'dp')), may hold values from -6 to 6
- clips_narrow: bfloat16 [64, 51, 768], P(('fsdp', 'dp')), may hold values from -6 to 6
- visible_wide: int32 [32, 102], P(('fsdp', 'dp')), may hold values from 0 to 511, as said below
- visible_narrow: int32 [64, 51], P(('fsdp', 'dp')), may hold values from 0 to 255, as said below
- shift_wide: int32 [32, 2], P(('fsdp', 'dp')), may hold values from 0 to 3
- shift_narrow: int32 [64], P(('fsdp', 'dp')), may hold values from 0 to 3
- enc_norm1: bfloat16 [768], P('fsdp'), may hold values from 0.5 to 1.5
- enc_qkv: bfloat16 [768, 2304], P('fsdp'), may hold values from -0.21875 to 0.21875
- enc_out: bfloat16 [768, 768], P('fsdp'), may hold values from -0.625 to 0.625
- enc_norm2: bfloat16 [768], P('fsdp'), may hold values from 0.5 to 1.5
- enc_up: bfloat16 [768, 3072], P('fsdp'), may hold values from -0.21875 to 0.21875
- enc_down: bfloat16 [3072, 768], P('fsdp'), may hold values from -0.109375 to 0.109375
- embed_proj: bfloat16 [768, 512], P('fsdp'), may hold values from -0.21875 to 0.21875
- mask_token: bfloat16 [512], P('fsdp'), may hold values from -4 to 4
- dec_norm1: bfloat16 [512], P('fsdp'), may hold values from 0.5 to 1.5
- dec_qkv: bfloat16 [512, 1536], P('fsdp'), may hold values from -0.25 to 0.25
- dec_out: bfloat16 [512, 512], P('fsdp'), may hold values from -0.5 to 0.5
- dec_norm2: bfloat16 [512], P('fsdp'), may hold values from 0.5 to 1.5
- dec_up: bfloat16 [512, 2048], P('fsdp'), may hold values from -0.25 to 0.25
- dec_down: bfloat16 [2048, 512], P('fsdp'), may hold values from -0.125 to 0.125
- cotan_wide: bfloat16 [32, 512, 512], P(('fsdp', 'dp')), may hold values from -6 to 6
- cotan_narrow: bfloat16 [64, 256, 512], P(('fsdp', 'dp')), may hold values from -6 to 6
Outputs:
- encoded_wide: bfloat16 [32, 102, 768], P(('fsdp', 'dp'))
- encoded_narrow: bfloat16 [64, 51, 768], P(('fsdp', 'dp'))
- decoded_wide: bfloat16 [32, 512, 512], P(('fsdp', 'dp'))
- decoded_narrow: bfloat16 [64, 256, 512], P(('fsdp', 'dp'))
- grad_wide: float32 [32, 102, 768], P(('fsdp', 'dp'))
- grad_narrow: float32 [64, 51, 768], P(('fsdp', 'dp'))
- grad_enc_norm1: float32 [768], P('fsdp')
- grad_enc_qkv: float32 [768, 2304], P('fsdp')
- grad_enc_out: float32 [768, 768], P('fsdp')
- grad_enc_norm2: float32 [768], P('fsdp')
- grad_enc_up: float32 [768, 3072], P('fsdp')
- grad_enc_down: float32 [3072, 768], P('fsdp')
- grad_embed_proj: float32 [768, 512], P('fsdp')
- grad_mask_token: float32 [512], P('fsdp')
- grad_dec_norm1: float32 [512], P('fsdp')
- grad_dec_qkv: float32 [512, 1536], P('fsdp')
- grad_dec_out: float32 [512, 512], P('fsdp')
- grad_dec_norm2: float32 [512], P('fsdp')
- grad_dec_up: float32 [512, 2048], P('fsdp')
- grad_dec_down: float32 [2048, 512], P('fsdp')
Inputs may be any that keep to these rules, and one draw needn't show every extreme that they name: `visible_wide`: each clip's 102 patch numbers are distinct and increasing. `visible_narrow`: each clip's 51 patch numbers are distinct and increasing.
All inputs are finite; a program needn't handle non-finite values.
Results may differ from a plain program's by a relative error of at most 0.024.
Values may be sent and summed in bfloat16 or wider, within the bound.
A program may use at most 192 MiB of HBM per device.

v0:
```python
import jax
import jax.numpy as jnp
from jax import lax
from jax.sharding import PartitionSpec as P

HEADS = 12
DHEADS = 16
TIME = 64
WIN = 4


EPS = 1e-06


def layer_norm(inputs, scales):
    center = jnp.mean(inputs, axis=-1, keepdims=True)
    shifted = inputs - center
    spread = jnp.mean(shifted * shifted, axis=-1, keepdims=True)
    return shifted * lax.rsqrt(spread + EPS) * scales


def gelu_exact(values):
    return jax.nn.gelu(values, approximate=False)


def matmul(former, latter):
    return jnp.dot(former, latter, preferred_element_type=jnp.float32)


def matmul_tn(former, latter):
    return lax.dot_general(
        former, latter, (((0,), (0,)), ((), ())), preferred_element_type=jnp.float32
    )


def matmul_nt(former, latter):
    return lax.dot_general(
        former, latter, (((1,), (1,)), ((), ())), preferred_element_type=jnp.float32
    )


def to_windows(canvas, shifts, columns):
    clip_count = canvas.shape[0]
    features = canvas.shape[-1]
    canvas = canvas.reshape(clip_count, TIME, columns, features)

    def to_roll_one(portion, offsets):
        portion = jnp.roll(portion, -offsets[0], axis=0)
        return jnp.roll(portion, -offsets[1], axis=1)

    canvas = jax.vmap(to_roll_one)(canvas, shifts)
    canvas = canvas.reshape(clip_count, TIME // WIN, WIN, columns // WIN, WIN, features)
    canvas = canvas.transpose(0, 1, 3, 2, 4, 5)
    return canvas.reshape(-1, WIN * WIN, features)


def from_windows(windows, shifts, columns):
    features = windows.shape[-1]
    clip_count = windows.shape[0] // (TIME // WIN * (columns // WIN))
    canvas = windows.reshape(clip_count, TIME // WIN, columns // WIN, WIN, WIN, features)
    canvas = canvas.transpose(0, 1, 3, 2, 4, 5).reshape(clip_count, TIME, columns, features)

    def from_roll_one(portion, offsets):
        portion = jnp.roll(portion, offsets[0], axis=0)
        return jnp.roll(portion, offsets[1], axis=1)

    canvas = jax.vmap(from_roll_one)(canvas, shifts)
    return canvas.reshape(clip_count, TIME * columns, features)


def plain_layout(clip_count, length):

    def arrange(portion):
        return portion.reshape(clip_count, length, portion.shape[-1])

    def restore(portion):
        return portion.reshape(clip_count * length, portion.shape[-1])

    return (clip_count * length, arrange, restore)


def window_layout(clip_count, columns, shifts):

    def arrange(portion):
        return to_windows(
            portion.reshape(clip_count, TIME * columns, portion.shape[-1]), shifts, columns
        )

    def restore(portion):
        return from_windows(portion, shifts, columns).reshape(
            clip_count * TIME * columns, portion.shape[-1]
        )

    return (clip_count * TIME * columns, arrange, restore)


def attend(queries, key_rows, values, num_heads):
    batches, length, features = queries.shape
    head_size = features // num_heads
    head_shape = (batches, length, num_heads, head_size)
    scores = jnp.einsum(
        "bqhd,bkhd->bhqk",
        queries.reshape(head_shape),
        key_rows.reshape(head_shape),
        preferred_element_type=jnp.float32,
    ) * head_size ** (-0.5)
    maximum = jnp.max(scores, axis=-1, keepdims=True)
    weights = jnp.exp(scores - maximum)
    totals = jnp.sum(weights, axis=-1, keepdims=True)
    shares = (weights / totals).astype(jnp.bfloat16)
    blended = jnp.einsum(
        "bhqk,bkhd->bqhd", shares, values.reshape(head_shape), preferred_element_type=jnp.float32
    )
    return (
        blended.astype(jnp.bfloat16).reshape(batches, length, features),
        maximum + jnp.log(totals),
    )


def attend_back(queries, key_rows, values, log_total, grad_blended, num_heads):
    batches, length, features = queries.shape
    head_size = features // num_heads
    scale = head_size ** (-0.5)
    head_shape = (batches, length, num_heads, head_size)
    queries = queries.reshape(head_shape)
    key_rows = key_rows.reshape(head_shape)
    values = values.reshape(head_shape)
    grad_blended = grad_blended.reshape(head_shape)
    scores = (
        jnp.einsum("bqhd,bkhd->bhqk", queries, key_rows, preferred_element_type=jnp.float32) * scale
    )
    shares = jnp.exp(scores - log_total)
    grad_values = jnp.einsum(
        "bhqk,bqhd->bkhd",
        shares.astype(jnp.bfloat16),
        grad_blended,
        preferred_element_type=jnp.float32,
    )
    grad_shares = jnp.einsum(
        "bqhd,bkhd->bhqk", grad_blended, values, preferred_element_type=jnp.float32
    )
    inner = jnp.sum(grad_shares * shares, axis=-1, keepdims=True)
    grad_scores = (shares * (grad_shares - inner)).astype(jnp.bfloat16)
    grad_queries = (
        jnp.einsum("bhqk,bkhd->bqhd", grad_scores, key_rows, preferred_element_type=jnp.float32)
        * scale
    )
    grad_keys = (
        jnp.einsum("bhqk,bqhd->bkhd", grad_scores, queries, preferred_element_type=jnp.float32)
        * scale
    )
    flat_shape = (batches, length, features)
    joined = jnp.concatenate(
        [
            grad_queries.reshape(flat_shape),
            grad_keys.reshape(flat_shape),
            grad_values.reshape(flat_shape),
        ],
        axis=-1,
    )
    return joined.astype(jnp.bfloat16)


def attention_forward(projected, layouts, num_heads):
    features = projected.shape[-1] // 3
    blended_parts = []
    log_totals = []
    offset = 0
    for row_count, arrange, restore in layouts:
        portion = arrange(projected[offset : offset + row_count])
        blended, log_total = attend(
            portion[..., :features],
            portion[..., features : 2 * features],
            portion[..., 2 * features :],
            num_heads,
        )
        blended_parts.append(restore(blended))
        log_totals.append(log_total)
        offset += row_count
    return (jnp.concatenate(blended_parts, 0), log_totals)


def attention_backward(projected, log_totals, grad_blended, layouts, num_heads):
    features = projected.shape[-1] // 3
    gradients = []
    offset = 0
    for position, (row_count, arrange, restore) in enumerate(layouts):
        portion = arrange(projected[offset : offset + row_count])
        grad_portion = arrange(grad_blended[offset : offset + row_count])
        joined = attend_back(
            portion[..., :features],
            portion[..., features : 2 * features],
            portion[..., 2 * features :],
            log_totals[position],
            grad_portion,
            num_heads,
        )
        gradients.append(restore(joined))
        offset += row_count
    return jnp.concatenate(gradients, 0)


def block_forward(inputs, weights, layouts, num_heads):
    gain_one, w_qkv, w_out, gain_two, w_up, w_down = weights
    normed = layer_norm(inputs, gain_one.astype(jnp.float32)).astype(jnp.bfloat16)
    projected = matmul(normed, w_qkv).astype(jnp.bfloat16)
    blended, log_totals = attention_forward(projected, layouts, num_heads)
    middle = inputs + matmul(blended, w_out)
    normed_two = layer_norm(middle, gain_two.astype(jnp.float32)).astype(jnp.bfloat16)
    raised = matmul(normed_two, w_up)
    active = gelu_exact(raised).astype(jnp.bfloat16)
    result = middle + matmul(active, w_down)
    return (
        result,
        (inputs, normed, projected, blended, log_totals, middle, normed_two, raised, active),
    )


def block_backward(grad_result, saved, weights, layouts, num_heads):
    inputs, normed, projected, blended, log_totals, middle, normed_two, raised, active = saved
    gain_one, w_qkv, w_out, gain_two, w_up, w_down = weights
    grad_low = grad_result.astype(jnp.bfloat16)
    grad_down = matmul_tn(active, grad_low)
    grad_active = matmul_nt(grad_low, w_down)
    gelu_value, gelu_pull = jax.vjp(gelu_exact, raised)
    grad_raised = gelu_pull(grad_active)[0].astype(jnp.bfloat16)
    grad_up = matmul_tn(normed_two, grad_raised)
    grad_normed_two = matmul_nt(grad_raised, w_up)
    norm_value, norm_pull = jax.vjp(layer_norm, middle, gain_two.astype(jnp.float32))
    grad_middle, grad_gain_two = norm_pull(grad_normed_two)
    grad_middle = grad_middle + grad_result
    grad_middle_low = grad_middle.astype(jnp.bfloat16)
    grad_out = matmul_tn(blended, grad_middle_low)
    grad_blended = matmul_nt(grad_middle_low, w_out).astype(jnp.bfloat16)
    grad_projected = attention_backward(projected, log_totals, grad_blended, layouts, num_heads)
    grad_qkv = matmul_tn(normed, grad_projected)
    grad_normed = matmul_nt(grad_projected, w_qkv)
    first_value, first_pull = jax.vjp(layer_norm, inputs, gain_one.astype(jnp.float32))
    grad_inputs, grad_gain_one = first_pull(grad_normed)
    return (
        grad_inputs + grad_middle,
        (grad_gain_one, grad_qkv, grad_out, grad_gain_two, grad_up, grad_down),
    )


def place(embedded, visible, filler, patches):
    clip_count = embedded.shape[0]
    canvas = jnp.broadcast_to(filler, (clip_count, patches, filler.shape[0]))
    clip_index = jnp.arange(clip_count, dtype=jnp.int32)[:, None]
    return canvas.at[clip_index, visible].set(embedded)


def masked_sum(grad_canvas, visible):
    clip_count, patches, features = grad_canvas.shape
    clip_index = jnp.arange(clip_count, dtype=jnp.int32)[:, None]
    masked = jnp.ones((clip_count, patches), jnp.float32).at[clip_index, visible].set(0.0)
    return jnp.sum(grad_canvas * masked[:, :, None], axis=(0, 1))


def pick_rows(grad_canvas, visible):
    clip_index = jnp.arange(grad_canvas.shape[0], dtype=jnp.int32)[:, None]
    return grad_canvas[clip_index, visible]


def local(
    clips_wide,
    clips_narrow,
    visible_wide,
    visible_narrow,
    shift_wide,
    shift_narrow,
    enc_norm1,
    enc_qkv,
    enc_out,
    enc_norm2,
    enc_up,
    enc_down,
    embed_proj,
    mask_token,
    dec_norm1,
    dec_qkv,
    dec_out,
    dec_norm2,
    dec_up,
    dec_down,
    cotan_wide,
    cotan_narrow,
):
    wide_count, wide_visible, model_width = clips_wide.shape
    narrow_count, narrow_visible, model_again = clips_narrow.shape
    wide_patches = cotan_wide.shape[1]
    narrow_patches = cotan_narrow.shape[1]
    decoder_width = cotan_wide.shape[2]
    wide_columns = wide_patches // TIME
    narrow_columns = narrow_patches // TIME
    narrow_shifts = jnp.stack([shift_narrow, jnp.zeros_like(shift_narrow)], axis=1)
    enc_layouts = [
        plain_layout(wide_count, wide_visible),
        plain_layout(narrow_count, narrow_visible),
    ]
    dec_layouts = [
        window_layout(wide_count, wide_columns, shift_wide),
        window_layout(narrow_count, narrow_columns, narrow_shifts),
    ]
    enc_full = (
        lax.all_gather(enc_norm1, "fsdp", axis=0, tiled=True),
        lax.all_gather(enc_qkv, "fsdp", axis=0, tiled=True),
        lax.all_gather(enc_out, "fsdp", axis=0, tiled=True),
        lax.all_gather(enc_norm2, "fsdp", axis=0, tiled=True),
        lax.all_gather(enc_up, "fsdp", axis=0, tiled=True),
        lax.all_gather(enc_down, "fsdp", axis=0, tiled=True),
        lax.all_gather(embed_proj, "fsdp", axis=0, tiled=True),
    )
    dec_full = (
        lax.all_gather(mask_token, "fsdp", axis=0, tiled=True),
        lax.all_gather(dec_norm1, "fsdp", axis=0, tiled=True),
        lax.all_gather(dec_qkv, "fsdp", axis=0, tiled=True),
        lax.all_gather(dec_out, "fsdp", axis=0, tiled=True),
        lax.all_gather(dec_norm2, "fsdp", axis=0, tiled=True),
        lax.all_gather(dec_up, "fsdp", axis=0, tiled=True),
        lax.all_gather(dec_down, "fsdp", axis=0, tiled=True),
    )
    enc_input = jnp.concatenate(
        [clips_wide.reshape(-1, model_width), clips_narrow.reshape(-1, model_width)], 0
    ).astype(jnp.float32)
    encoded, enc_saved = block_forward(enc_input, enc_full[:6], enc_layouts, HEADS)
    encoded_low = encoded.astype(jnp.bfloat16)
    embedded = matmul(encoded_low, enc_full[6])
    wide_rows = wide_count * wide_visible
    filler = dec_full[0].astype(jnp.float32)
    canvas_wide = place(
        embedded[:wide_rows].reshape(wide_count, wide_visible, decoder_width),
        visible_wide,
        filler,
        wide_patches,
    )
    canvas_narrow = place(
        embedded[wide_rows:].reshape(narrow_count, narrow_visible, decoder_width),
        visible_narrow,
        filler,
        narrow_patches,
    )
    dec_input = jnp.concatenate(
        [canvas_wide.reshape(-1, decoder_width), canvas_narrow.reshape(-1, decoder_width)], 0
    )
    decoded, dec_saved = block_forward(dec_input, dec_full[1:], dec_layouts, DHEADS)
    decoded_low = decoded.astype(jnp.bfloat16)
    grad_decoded = jnp.concatenate(
        [cotan_wide.reshape(-1, decoder_width), cotan_narrow.reshape(-1, decoder_width)], 0
    ).astype(jnp.float32)
    dec_back = (
        lax.all_gather(dec_norm1, "fsdp", axis=0, tiled=True),
        lax.all_gather(dec_qkv, "fsdp", axis=0, tiled=True),
        lax.all_gather(dec_out, "fsdp", axis=0, tiled=True),
        lax.all_gather(dec_norm2, "fsdp", axis=0, tiled=True),
        lax.all_gather(dec_up, "fsdp", axis=0, tiled=True),
        lax.all_gather(dec_down, "fsdp", axis=0, tiled=True),
    )
    dec_saved = block_forward(dec_input, dec_back, dec_layouts, DHEADS)[1]
    grad_canvas, dec_grads = block_backward(grad_decoded, dec_saved, dec_back, dec_layouts, DHEADS)
    wide_patch_rows = wide_count * wide_patches
    grad_canvas_wide = grad_canvas[:wide_patch_rows].reshape(
        wide_count, wide_patches, decoder_width
    )
    grad_canvas_narrow = grad_canvas[wide_patch_rows:].reshape(
        narrow_count, narrow_patches, decoder_width
    )
    grad_filler = masked_sum(grad_canvas_wide, visible_wide) + masked_sum(
        grad_canvas_narrow, visible_narrow
    )
    grad_embedded = jnp.concatenate(
        [
            pick_rows(grad_canvas_wide, visible_wide).reshape(-1, decoder_width),
            pick_rows(grad_canvas_narrow, visible_narrow).reshape(-1, decoder_width),
        ],
        0,
    ).astype(jnp.bfloat16)
    enc_back = (
        lax.all_gather(enc_norm1, "fsdp", axis=0, tiled=True),
        lax.all_gather(enc_qkv, "fsdp", axis=0, tiled=True),
        lax.all_gather(enc_out, "fsdp", axis=0, tiled=True),
        lax.all_gather(enc_norm2, "fsdp", axis=0, tiled=True),
        lax.all_gather(enc_up, "fsdp", axis=0, tiled=True),
        lax.all_gather(enc_down, "fsdp", axis=0, tiled=True),
        lax.all_gather(embed_proj, "fsdp", axis=0, tiled=True),
    )
    grad_proj = matmul_tn(encoded_low, grad_embedded)
    grad_encoded = matmul_nt(grad_embedded, enc_back[6])
    grad_input, enc_grads = block_backward(
        grad_encoded, enc_saved, enc_back[:6], enc_layouts, HEADS
    )
    all_shares = (
        lax.psum_scatter(enc_grads[0], ("fsdp", "dp"), scatter_dimension=0, tiled=True),
        lax.psum_scatter(enc_grads[1], ("fsdp", "dp"), scatter_dimension=0, tiled=True),
        lax.psum_scatter(enc_grads[2], ("fsdp", "dp"), scatter_dimension=0, tiled=True),
        lax.psum_scatter(enc_grads[3], ("fsdp", "dp"), scatter_dimension=0, tiled=True),
        lax.psum_scatter(enc_grads[4], ("fsdp", "dp"), scatter_dimension=0, tiled=True),
        lax.psum_scatter(enc_grads[5], ("fsdp", "dp"), scatter_dimension=0, tiled=True),
        lax.psum_scatter(grad_proj, ("fsdp", "dp"), scatter_dimension=0, tiled=True),
        lax.psum_scatter(grad_filler, ("fsdp", "dp"), scatter_dimension=0, tiled=True),
        lax.psum_scatter(dec_grads[0], ("fsdp", "dp"), scatter_dimension=0, tiled=True),
        lax.psum_scatter(dec_grads[1], ("fsdp", "dp"), scatter_dimension=0, tiled=True),
        lax.psum_scatter(dec_grads[2], ("fsdp", "dp"), scatter_dimension=0, tiled=True),
        lax.psum_scatter(dec_grads[3], ("fsdp", "dp"), scatter_dimension=0, tiled=True),
        lax.psum_scatter(dec_grads[4], ("fsdp", "dp"), scatter_dimension=0, tiled=True),
        lax.psum_scatter(dec_grads[5], ("fsdp", "dp"), scatter_dimension=0, tiled=True),
    )
    enc_shares = all_shares[:7]
    dec_shares = all_shares[7:]
    totals = (
        lax.all_gather(enc_shares[0].astype(jnp.bfloat16), "dp", axis=0, tiled=True).astype(
            jnp.float32
        ),
        lax.all_gather(enc_shares[1].astype(jnp.bfloat16), "dp", axis=0, tiled=True).astype(
            jnp.float32
        ),
        lax.all_gather(enc_shares[2].astype(jnp.bfloat16), "dp", axis=0, tiled=True).astype(
            jnp.float32
        ),
        lax.all_gather(enc_shares[3].astype(jnp.bfloat16), "dp", axis=0, tiled=True).astype(
            jnp.float32
        ),
        lax.all_gather(enc_shares[4].astype(jnp.bfloat16), "dp", axis=0, tiled=True).astype(
            jnp.float32
        ),
        lax.all_gather(enc_shares[5].astype(jnp.bfloat16), "dp", axis=0, tiled=True).astype(
            jnp.float32
        ),
        lax.all_gather(enc_shares[6].astype(jnp.bfloat16), "dp", axis=0, tiled=True).astype(
            jnp.float32
        ),
        lax.all_gather(dec_shares[0].astype(jnp.bfloat16), "dp", axis=0, tiled=True).astype(
            jnp.float32
        ),
        lax.all_gather(dec_shares[1].astype(jnp.bfloat16), "dp", axis=0, tiled=True).astype(
            jnp.float32
        ),
        lax.all_gather(dec_shares[2].astype(jnp.bfloat16), "dp", axis=0, tiled=True).astype(
            jnp.float32
        ),
        lax.all_gather(dec_shares[3].astype(jnp.bfloat16), "dp", axis=0, tiled=True).astype(
            jnp.float32
        ),
        lax.all_gather(dec_shares[4].astype(jnp.bfloat16), "dp", axis=0, tiled=True).astype(
            jnp.float32
        ),
        lax.all_gather(dec_shares[5].astype(jnp.bfloat16), "dp", axis=0, tiled=True).astype(
            jnp.float32
        ),
        lax.all_gather(dec_shares[6].astype(jnp.bfloat16), "dp", axis=0, tiled=True).astype(
            jnp.float32
        ),
    )
    encoded_wide = encoded_low[:wide_rows].reshape(wide_count, wide_visible, model_width)
    encoded_narrow = encoded_low[wide_rows:].reshape(narrow_count, narrow_visible, model_width)
    decoded_wide = decoded_low[:wide_patch_rows].reshape(wide_count, wide_patches, decoder_width)
    decoded_narrow = decoded_low[wide_patch_rows:].reshape(
        narrow_count, narrow_patches, decoder_width
    )
    grad_wide = grad_input[:wide_rows].reshape(wide_count, wide_visible, model_width)
    grad_narrow = grad_input[wide_rows:].reshape(narrow_count, narrow_visible, model_width)
    return (
        encoded_wide,
        encoded_narrow,
        decoded_wide,
        decoded_narrow,
        grad_wide,
        grad_narrow,
        totals[0],
        totals[1],
        totals[2],
        totals[3],
        totals[4],
        totals[5],
        totals[6],
        totals[7],
        totals[8],
        totals[9],
        totals[10],
        totals[11],
        totals[12],
        totals[13],
    )


def solution(mesh):
    return jax.shard_map(
        local,
        mesh=mesh,
        in_specs=(
            P(("fsdp", "dp"), None, None),
            P(("fsdp", "dp"), None, None),
            P(("fsdp", "dp"), None),
            P(("fsdp", "dp"), None),
            P(("fsdp", "dp"), None),
            P(("fsdp", "dp")),
            P("fsdp"),
            P("fsdp", None),
            P("fsdp", None),
            P("fsdp"),
            P("fsdp", None),
            P("fsdp", None),
            P("fsdp", None),
            P("fsdp"),
            P("fsdp"),
            P("fsdp", None),
            P("fsdp", None),
            P("fsdp"),
            P("fsdp", None),
            P("fsdp", None),
            P(("fsdp", "dp"), None, None),
            P(("fsdp", "dp"), None, None),
        ),
        out_specs=(
            P(("fsdp", "dp"), None, None),
            P(("fsdp", "dp"), None, None),
            P(("fsdp", "dp"), None, None),
            P(("fsdp", "dp"), None, None),
            P(("fsdp", "dp"), None, None),
            P(("fsdp", "dp"), None, None),
            P("fsdp"),
            P("fsdp", None),
            P("fsdp", None),
            P("fsdp"),
            P("fsdp", None),
            P("fsdp", None),
            P("fsdp", None),
            P("fsdp"),
            P("fsdp"),
            P("fsdp", None),
            P("fsdp", None),
            P("fsdp"),
            P("fsdp", None),
            P("fsdp", None),
        ),
        check_vma=False,
    )
```

profile of v0, /device:TPU:11, one launch (start us, length us, event | category | flops | bytes accessed | tf_op | source)
XLA Modules:
  0.0 1709.9 jit_solution(13681746422270983866)
XLA Ops:
  27.2 26.1 %all-reduce.21 = (bf16[512]{0:T(512)(128)(2,1)S(1)}, bf16[768]{0:T(1024)(128)(2,1)S(1)}, bf16[768]{0:T(1024)(128)(2,1)S(1)}, bf16[512]{0:T(512)(128)(2,1)S(1)}, bf16[512]{0:T(512)(128)(2,1)S(1)}) all-reduce(bf16[512]{0:T(512)(128)(2,1)S(1)} %dynamic-update-slice.6, ...), channel_id=1, replica_groups=mesh['fsdp'=16,'dp'=2] {'fsdp'}, use_global_device_ids=true, to_apply=%add.7 | all-reduce | flops 3072 | bytes 12288
  58.1 40.6 %all_gather.107 = bf16[512,512]{1,0:T(8,128)(2,1)} all-gather(bf16[32,512]{1,0:T(8,128)(2,1)S(1)} %copy-done.98), channel_id=1, replica_groups=mesh['fsdp'=16,'dp'=2] {'fsdp'}, dimensions={0}, use_global_device_ids=true | all-gather | bytes 557056 | tf_op jit(solution)/shard_map/all_gather | solution.py:318
  98.7 34.7 %all_gather.104 = bf16[768,512]{1,0:T(8,128)(2,1)S(1)} all-gather(bf16[48,512]{1,0:T(8,128)(2,1)S(1)} %copy-done.91), channel_id=1, replica_groups=mesh['fsdp'=16,'dp'=2] {'fsdp'}, dimensions={0}, use_global_device_ids=true | all-gather | bytes 835584 | tf_op jit(solution)/shard_map/all_gather | solution.py:312
  146.5 80.9 %all-gather.12.cloned.1.call-done = bf16[768,3072]{1,0:T(8,128)(2,1)} async-done(((bf16[48,3072]{1,0:T(8,128)(2,1)}), bf16[768,3072]{1,0:T(8,128)(2,1)}) %all-gather.12.cloned.1.call-update) | async-done | bytes 4718608 | tf_op jit(solution)/shard_map/all_gather | solution.py:310
  227.4 9.4 multiply_convert_fusion.7
  236.8 72.4 %all-gather.14.cloned.1.call-done = bf16[3072,768]{1,0:T(8,128)(2,1)} async-done(((bf16[192,768]{1,0:T(8,128)(2,1)}), bf16[3072,768]{1,0:T(8,128)(2,1)}) %all-gather.14.cloned.1.call-update) | async-done | bytes 4718608 | tf_op jit(solution)/shard_map/all_gather | solution.py:311
  315.3 6.5 scatter_fusion
  322.5 45.5 %all-gather.16.cloned.1.call-done = bf16[512,1536]{1,0:T(8,128)(2,1)} async-done(((bf16[32,1536]{1,0:T(8,128)(2,1)}), bf16[512,1536]{1,0:T(8,128)(2,1)}) %all-gather.16.cloned.1.call-update) | async-done | bytes 1572880 | tf_op jit(solution)/shard_map/all_gather | solution.py:317
  466.8 23.9 %multiply_convert_fusion = (bf16[1024,2048]{1,0:T(8,128)(2,1)}, f32[1024,2048]{1,0:T(8,128)}, f32[1024,2048]{1,0:T(8,128)}) fusion(bf16[512,2048]{1,0:T(8,128)(2,1)} %all-gather.18.cloned.1.call-done, f32[1024,512]{1,0:T(8,128)S(1)} %get-tuple-element.235, f32[512]{0:T(512)S(1)} %convert_element_type.279, f32[1024]{0:T(1024)S(1)} %fusion.128, ...), kind=kOutput, calls=%fused_computation.17 | convolution fusion | flops 2285895680 | bytes 25176064 | tf_op jit(solution)/shard_map/dot_general | solution.py:27
  493.1 9.3 add_convert_fusion
  627.8 9.5 maximum_maximum_fusion
  706.2 6.5 fusion.157
  712.8 6.7 fusion.166
  748.7 6.5 fusion.163
  781.0 39.3 %all-reduce.20 = (bf16[768]{0:T(1024)(128)(2,1)S(1)}, bf16[768]{0:T(1024)(128)(2,1)S(1)}, bf16[512]{0:T(512)(128)(2,1)S(1)}, bf16[512]{0:T(512)(128)(2,1)S(1)}, bf16[512]{0:T(512)(128)(2,1)S(1)}) all-reduce(f32[768]{0:T(1024)S(1)} %get-tuple-element.160, ...), channel_id=2, replica_groups=mesh['fsdp'=16,'dp'=2] {'fsdp','dp'}, use_global_device_ids=true, to_apply=%region_31.40.clone | all-reduce | flops 3072 | bytes 18432
  844.2 63.3 %reduce-scatter.12.cloned.1.call-done = f32[24,768]{1,0:T(8,128)} async-done(((f32[768,768]{1,0:T(8,128)}), f32[24,768]{1,0:T(8,128)}) %reduce-scatter.12.cloned.1.call-update) | async-done | bytes 73744 | tf_op jit(solution)/shard_map/reduce_scatter | solution.py:395
  912.8 100.6 %reduce-scatter.20.cloned.1.call-done = f32[16,1536]{1,0:T(8,128)} async-done(((f32[512,1536]{1,0:T(8,128)}), f32[16,1536]{1,0:T(8,128)}) %reduce-scatter.20.cloned.1.call-update) | async-done | bytes 98320 | tf_op jit(solution)/shard_map/reduce_scatter | solution.py:402
  1018.8 109.3 %reduce-scatter.26.cloned.1.call-done = f32[64,512]{1,0:T(8,128)} async-done(((f32[2048,512]{1,0:T(8,128)}), f32[64,512]{1,0:T(8,128)}) %reduce-scatter.26.cloned.1.call-update) | async-done | bytes 131088 | tf_op jit(solution)/shard_map/reduce_scatter | solution.py:406
  1129.0 7.3 all_gather.124
  1137.0 130.4 %reduce-scatter.24.cloned.1.call-done = f32[16,2048]{1,0:T(8,128)} async-done(((f32[512,2048]{1,0:T(8,128)}), f32[16,2048]{1,0:T(8,128)}) %reduce-scatter.24.cloned.1.call-update) | async-done | bytes 131088 | tf_op jit(solution)/shard_map/reduce_scatter | solution.py:405
  1268.4 7.2 all_gather.123
  1276.2 139.2 %reduce-scatter.10.cloned.1.call-done = f32[24,2304]{1,0:T(8,128)} async-done(((f32[768,2304]{1,0:T(8,128)}), f32[24,2304]{1,0:T(8,128)}) %reduce-scatter.10.cloned.1.call-update) | async-done | bytes 221200 | tf_op jit(solution)/shard_map/reduce_scatter | solution.py:394
  1421.2 135.6 %reduce-scatter.14.cloned.1.call-done = f32[24,3072]{1,0:T(8,128)} async-done(((f32[768,3072]{1,0:T(8,128)}), f32[24,3072]{1,0:T(8,128)}) %reduce-scatter.14.cloned.1.call-update) | async-done | bytes 294928 | tf_op jit(solution)/shard_map/reduce_scatter | solution.py:397
  1562.7 134.5 %reduce-scatter.16.cloned.1.call-done = f32[96,768]{1,0:T(8,128)} async-done(((f32[3072,768]{1,0:T(8,128)}), f32[96,768]{1,0:T(8,128)}) %reduce-scatter.16.cloned.1.call-update) | async-done | bytes 294928 | tf_op jit(solution)/shard_map/reduce_scatter | solution.py:398
  (560 shorter events, 440.6 us)
Async XLA Ops:
  7.2 126.3 %copy-start.43 = (bf16[1,102,768]{2,1,0:T(8,128)(2,1)S(1)}, bf16[1,102,768]{2,1,0:T(8,128)(2,1)}, u32[]{:S(2)}) copy-start(bf16[1,102,768]{2,1,0:T(8,128)(2,1)} %param.38) | copy-start | bytes 470020
  7.2 91.5 %copy-start.91 = (bf16[48,512]{1,0:T(8,128)(2,1)S(1)}, bf16[48,512]{1,0:T(8,128)(2,1)}, u32[]{:S(2)}) copy-start(bf16[48,512]{1,0:T(8,128)(2,1)} %param.50) | copy-start | bytes 147460
  7.2 126.2 %all-gather.8.cloned.1.call-start = ((), (), s32[]{:S(2)}) async-start(), calls=%async_computation.9 | async-start | bytes 3760128 | tf_op jit(solution)/shard_map/all_gather | solution.py:307
  8.0 136.4 %all-gather.10.cloned.1.call-start = ((), (), s32[]{:S(2)}) async-start(), calls=%async_computation.10 | async-start | bytes 1253376 | tf_op jit(solution)/shard_map/all_gather | solution.py:308
  8.7 218.7 %all-gather.12.cloned.1.call-start = ((), (), s32[]{:S(2)}) async-start(), calls=%async_computation.11 | async-start | bytes 5013504 | tf_op jit(solution)/shard_map/all_gather | solution.py:310
  9.4 299.7 %all-gather.14.cloned.1.call-start = ((), (), s32[]{:S(2)}) async-start(), calls=%async_computation.12 | async-start | bytes 5013504 | tf_op jit(solution)/shard_map/all_gather | solution.py:311
  10.0 357.9 %all-gather.16.cloned.1.call-start = ((), (), s32[]{:S(2)}) async-start(), calls=%async_computation.13 | async-start | bytes 1671168 | tf_op jit(solution)/shard_map/all_gather | solution.py:317
  10.6 456.2 %all-gather.18.cloned.1.call-start = ((), (), s32[]{:S(2)}) async-start(), calls=%async_computation.14 | async-start | bytes 2228224 | tf_op jit(solution)/shard_map/all_gather | solution.py:320
  11.2 481.9 %all-gather.20.cloned.1.call-start = ((), (), s32[]{:S(2)}) async-start(), calls=%async_computation.15 | async-start | bytes 2228224 | tf_op jit(solution)/shard_map/all_gather | solution.py:321
  11.9 825.7 %reduce-scatter.22.cloned.1.call-start = ((), (), s32[]{:S(2)}) async-start(), calls=%async_computation.22 | async-start | bytes 1081344 | tf_op jit(solution)/shard_map/reduce_scatter | solution.py:403
  22.3 291.3 %copy-start.116 = (s32[102]{0:T(128)}, s32[102]{0:T(128)S(1)}, u32[]{:S(2)}) copy-start(s32[102]{0:T(128)S(1)} %get-tuple-element.216) | copy-start | bytes 1228
  53.3 314.6 %copy-start.111 = (f32[512]{0:T(512)}, f32[512]{0:T(512)S(1)}, u32[]{:S(2)}) copy-start(f32[512]{0:T(512)S(1)} %convert_element_type.270) | copy-start | bytes 6148
  54.8 260.5 %copy-start.4 = (s32[102]{0:T(128)}, s32[102]{0:T(128)S(1)}, u32[]{:S(2)}) copy-start(s32[102]{0:T(128)S(1)} %reshape.761) | copy-start | bytes 1228
  54.8 172.6 %copy-start.79 = (f32[768]{0:T(1024)}, f32[768]{0:T(1024)S(1)}, u32[]{:S(2)}) copy-start(f32[768]{0:T(1024)S(1)} %convert_element_type.265) | copy-start | bytes 9220
  133.5 179.2 %copy-start.31 = (bf16[768,512]{1,0:T(8,128)(2,1)}, bf16[768,512]{1,0:T(8,128)(2,1)S(1)}, u32[]{:S(2)}) copy-start(bf16[768,512]{1,0:T(8,128)(2,1)S(1)} %all_gather.104) | copy-start | bytes 2359300
  146.2 163.0 %copy-start.34 = (f32[204,768]{1,0:T(8,128)}, f32[204,768]{1,0:T(8,128)S(1)}, u32[]{:S(2)}) copy-start(f32[204,768]{1,0:T(8,128)S(1)} %get-tuple-element.228) | copy-start | bytes 1880068
  571.7 269.2 %reduce-scatter.18.cloned.1.call-start = ((), (), s32[]{:S(2)}) async-start(), calls=%async_computation.20 | async-start | bytes 1622016 | tf_op jit(solution)/shard_map/reduce_scatter | solution.py:399
  684.4 223.1 %reduce-scatter.12.cloned.1.call-start = ((), (), s32[]{:S(2)}) async-start(), calls=%async_computation.17 | async-start | bytes 2433024 | tf_op jit(solution)/shard_map/reduce_scatter | solution.py:395
  699.1 314.3 %reduce-scatter.20.cloned.1.call-start = ((), (), s32[]{:S(2)}) async-start(), calls=%async_computation.21 | async-start | bytes 3244032 | tf_op jit(solution)/shard_map/reduce_scatter | solution.py:402
  705.0 423.1 %reduce-scatter.26.cloned.1.call-start = ((), (), s32[]{:S(2)}) async-start(), calls=%async_computation.24 | async-start | bytes 4325376 | tf_op jit(solution)/shard_map/reduce_scatter | solution.py:406
  712.7 554.7 %reduce-scatter.24.cloned.1.call-start = ((), (), s32[]{:S(2)}) async-start(), calls=%async_computation.23 | async-start | bytes 4325376 | tf_op jit(solution)/shard_map/reduce_scatter | solution.py:405
  719.6 695.9 %reduce-scatter.10.cloned.1.call-start = ((), (), s32[]{:S(2)}) async-start(), calls=%async_computation.16 | async-start | bytes 7299072 | tf_op jit(solution)/shard_map/reduce_scatter | solution.py:394
  747.7 809.1 %reduce-scatter.14.cloned.1.call-start = ((), (), s32[]{:S(2)}) async-start(), calls=%async_computation.18 | async-start | bytes 9732096 | tf_op jit(solution)/shard_map/reduce_scatter | solution.py:397
  755.3 941.9 %reduce-scatter.16.cloned.1.call-start = ((), (), s32[]{:S(2)}) async-start(), calls=%async_computation.19 | async-start | bytes 9732096 | tf_op jit(solution)/shard_map/reduce_scatter | solution.py:398
  (111 other events, 1395.2 us)
Sparse Core Ops, SparseCore 0:
  10.9 72.2 all-gather.7
  85.9 58.4 all-gather.9
  147.2 80.1 all-gather.11
  230.1 79.0 all-gather.13
  311.8 56.0 all-gather.15
  370.6 60.3 all-gather.17
  433.7 59.3 all-gather.19
  571.8 104.8 reduce-scatter.21
  684.5 118.8 reduce-scatter.17
  809.4 98.0 reduce-scatter.11
  912.9 100.4 reduce-scatter.19
  1015.6 112.4 reduce-scatter.25
  1130.4 137.0 reduce-scatter.23
  1273.0 142.4 reduce-scatter.9
  1422.2 134.5 reduce-scatter.13
  1562.5 134.6 reduce-scatter.15
where the time goes:
time: 1720 us; the launch traced here: 1710 us
  waiting for transfers between devices  1020 us (59%)
  local copies, waits for them, and re-layouts  227 us (13%)
  matrix products  183 us (11%)
  blocking collectives  182 us (11%)
  other arithmetic  73.6 us (4%)
  between operations  24 us (1%)
    reduce_scatter x1, waiting for transfers between devices, local(): lax.psum_scatter(enc_grads[1], ('fsdp', 'dp'), scatter_dimension=0, tiled...  139 us
    reduce_scatter x1, waiting for transfers between devices, local(): lax.psum_scatter(enc_grads[4], ('fsdp', 'dp'), scatter_dimension=0, tiled...  136 us
    reduce_scatter x1, waiting for transfers between devices, local(): lax.psum_scatter(enc_grads[5], ('fsdp', 'dp'), scatter_dimension=0, tiled...  135 us
    reduce_scatter x1, waiting for transfers between devices, local(): lax.psum_scatter(dec_grads[4], ('fsdp', 'dp'), scatter_dimension=0, tiled...  130 us
    reduce_scatter x1, waiting for transfers between devices, local(): lax.psum_scatter(dec_grads[5], ('fsdp', 'dp'), scatter_dimension=0, tiled...  109 us
    reduce_scatter x1, waiting for transfers between devices, local(): lax.psum_scatter(dec_grads[1], ('fsdp', 'dp'), scatter_dimension=0, tiled...  101 us
    all_gather x1, waiting for transfers between devices, local(): lax.all_gather(enc_up, 'fsdp', axis=0, tiled=True)  80.9 us
    all_gather x1, waiting for transfers between devices, local(): lax.all_gather(enc_down, 'fsdp', axis=0, tiled=True)  72.4 us
  transfers between devices with their start and end apart: 16, of which 12 were waited for; matrix products, arithmetic and copies ran while one was open for 23% of the time, Pallas kernels for 0%

commit v1 on v0

--- a/solution.py
+++ b/solution.py
@@ -1,6 +1,10 @@
+import functools
+
 import jax
 import jax.numpy as jnp
 from jax import lax
+from jax.experimental import pallas as pl
+from jax.experimental.pallas import tpu as pltpu
 from jax.sharding import PartitionSpec as P
 
 HEADS = 12
@@ -10,6 +14,338 @@
 
 
 EPS = 1e-06
+
+
+MESH = pl.DeviceIdType.MESH
+
+
+def slots():
+    out=[]
+    for bx in (0,1):
+        for by in (0,1):
+            for sgn in (0,1,-1):
+                if (bx,by,sgn)!=(0,0,0): out.append((bx,by,sgn))
+    return out
+
+def forwards(order,bx,by,sgn):
+    differs={'x':bx,'y':by,'z':int(sgn!=0)}
+    last=max([j for j,d in enumerate(order) if differs[d]],default=-1)
+    dirs=[]
+    for j,d in enumerate(order):
+        if j>last:
+            dirs += ['u','d'] if d=='z' else [d]
+    if last>=0 and order[last]=='z':
+        dirs.append('u' if sgn<0 else 'd')
+    return dirs
+
+def ag_kernel(nz, pieces, nw, *refs):
+    ins=refs[:nw]; outs=refs[nw:2*nw]
+    send, recv, sib_send, sib_recv, loc = refs[2*nw:]
+    f=lax.axis_index("fsdp"); c=lax.axis_index("dp")
+    z=f//4; y=(f//2)%2; x=f%2
+    xn=(f+1-2*x, c); yn=(f+2-4*y, c); up=(f+4,c); dn=(f-4,c); sib=(f,1-c)
+    bar=pltpu.get_barrier_semaphore()
+    def sig(dev): pl.semaphore_signal(bar,inc=1,device_id=dev,device_id_type=MESH)
+    sig(xn); sig(yn); sig(sib)
+    @pl.when(z<nz-1)
+    def _(): sig(up)
+    @pl.when(z>0)
+    def _(): sig(dn)
+    pl.semaphore_wait(bar, 3+(z<nz-1).astype(jnp.int32)+(z>0).astype(jnp.int32))
+    dest={'x':xn,'y':yn,'u':up,'d':dn}
+    ok={'x':None,'y':None,'u':z<nz-1,'d':z>0}
+    code={'x':0,'y':1,'u':2,'d':3}
+    def rows(w): return ins[w].shape[0]
+    def region(i, s, half):
+        w,c0,cols,order,share=pieces[i]
+        r=rows(w)
+        n=ins[w].shape[1]
+        col=c0 if not share else pl.multiple_of(half*(n//2)+c0,128)
+        return outs[w].at[pl.ds(pl.multiple_of(s*r,r),r), pl.ds(col,cols)]
+    def own(i):
+        w,c0,cols,order,share=pieces[i]
+        n=ins[w].shape[1]
+        col=c0 if not share else pl.multiple_of(c*(n//2)+c0,128)
+        return ins[w].at[:, pl.ds(col,cols)]
+    def remote(i,s,src,d):
+        return pltpu.make_async_remote_copy(src_ref=src,dst_ref=region(i,s,c),send_sem=send.at[i,s,code[d]],recv_sem=recv.at[i,s],device_id=dest[d],device_id_type=MESH)
+    def sibling(i,s):
+        return pltpu.make_async_remote_copy(src_ref=region(i,s,c),dst_ref=region(i,s,c),send_sem=sib_send.at[i,s],recv_sem=sib_recv.at[i,s],device_id=sib,device_id_type=MESH)
+    def go(i,s,src,dirs):
+        for d in dirs:
+            if ok[d] is None: remote(i,s,src,d).start()
+            else:
+                pl.when(ok[d])(lambda d=d: remote(i,s,src,d).start())
+    def wait_sends(i,s,src,dirs):
+        for d in dirs:
+            if ok[d] is None: remote(i,s,src,d).wait_send()
+            else:
+                pl.when(ok[d])(lambda d=d: remote(i,s,src,d).wait_send())
+    locals_=[]
+    for i in range(len(pieces)):
+        go(i,f,own(i),forwards(pieces[i][3],0,0,0))
+    for w in range(nw):
+        r=rows(w)
+        cp=pltpu.make_async_copy(ins[w],outs[w].at[pl.ds(pl.multiple_of(f*r,r),r)],loc.at[w]); cp.start(); locals_.append(cp)
+    def each(h, i, action):
+        for bx,by,sgn in slots():
+            k=h-bx-by
+            zs=z+sgn*k
+            if sgn==0: valid=k==0
+            else: valid=(k>=1)&(zs>=0)&(zs<nz)
+            s=zs*4+(y+by-2*by*y)*2+(x+bx-2*bx*x)
+            pl.when(valid)(lambda s=s,bx=bx,by=by,sgn=sgn: action(i,s,forwards(pieces[i][3],bx,by,sgn)))
+    def step(i,s,dirs):
+        remote(i,s,region(i,s,c),'x').wait_recv()
+        go(i,s,region(i,s,c),dirs)
+        if pieces[i][4]: sibling(i,s).start()
+    def fin(i,s,dirs):
+        wait_sends(i,s,region(i,s,c),dirs)
+        if pieces[i][4]:
+            sibling(i,s).wait_send()
+            pltpu.make_async_remote_copy(src_ref=region(i,s,1-c),dst_ref=region(i,s,1-c),send_sem=sib_send.at[i,s],recv_sem=sib_recv.at[i,s],device_id=sib,device_id_type=MESH).wait_recv()
+    @pl.loop(1,nz+2)
+    def _(h):
+        for i in range(len(pieces)):
+            each(h,i,step)
+    for i in range(len(pieces)):
+        wait_sends(i,f,own(i),forwards(pieces[i][3],0,0,0))
+    for cp in locals_: cp.wait()
+    @pl.loop(1,nz+2)
+    def _(h):
+        for i in range(len(pieces)):
+            each(h,i,fin)
+
+def all_gather(shards, pieces, nz, cid=1):
+    nw=len(shards); npc=len(pieces); n=nz*4
+    return pl.pallas_call(functools.partial(ag_kernel,nz,pieces,nw),
+        out_shape=[jax.ShapeDtypeStruct((s.shape[0]*n,s.shape[1]),s.dtype) for s in shards],
+        in_specs=[pl.BlockSpec(memory_space=pl.ANY)]*nw,
+        out_specs=[pl.BlockSpec(memory_space=pl.ANY)]*nw,
+        scratch_shapes=[pltpu.SemaphoreType.DMA((npc,n,4)),pltpu.SemaphoreType.DMA((npc,n)),pltpu.SemaphoreType.DMA((npc,n)),pltpu.SemaphoreType.DMA((npc,n)),pltpu.SemaphoreType.DMA((nw,))],
+        compiler_params=pltpu.CompilerParams(collective_id=cid,has_side_effects=True),
+        name="gather_weights")(*shards)
+
+def slot_count(order, d, nz):
+    size={'x':2,'y':2,'z':nz}
+    j=order.index('z' if d in 'ud' else d)
+    k=1
+    for e in order[:j]: k*=size[e]
+    return k*(nz+1) if d in 'ud' else k
+
+def slot_index(order, d, nz, pos):
+    size={'x':2,'y':2,'z':nz}
+    j=order.index('z' if d in 'ud' else d)
+    k=0
+    for e in order[:j]: k=k*size[e]+pos[e]
+    if d in 'ud': k=k*(nz+1)+pos['z']+(1 if d=='d' else 0)
+    return k
+
+LEAD = 0
+def rs_kernel(nz, pieces, nw, *refs):
+    ins=refs[:nw]; vec=refs[nw]; outs=refs[nw+1:2*nw+1]; vout=refs[2*nw+1]
+    rest=list(refs[2*nw+2:])
+    npc=len(pieces)
+    own=[rest.pop(0) for _ in range(npc)]
+    sibb=[rest.pop(0) for _ in range(npc)]
+    rbuf=[[rest.pop(0) for _ in range(3)] for _ in range(npc)]
+    res=[rest.pop(0) for _ in range(npc)]
+    vbuf, own_sem, sib_send, sib_recv, send, recv, res_sem, res_send, res_recv, vsend, vrecv = rest
+    f=lax.axis_index("fsdp"); c=lax.axis_index("dp")
+    z=f//4; y=(f//2)%2; x=f%2
+    bits=(nz*4).bit_length()-1
+    def flip(b): return f+(1<<b)*(1-2*((f//(1<<b))%2))
+    xn=(flip(0), c); yn=(flip(1), c); up=(f+4,c); dn=(f-4,c); sib=(f,1-c)
+    bar=pltpu.get_barrier_semaphore()
+    def sig(dev): pl.semaphore_signal(bar,inc=1,device_id=dev,device_id_type=MESH)
+    sig(xn); sig(yn); sig(sib)
+    @pl.when(z<nz-1)
+    def _(): sig(up)
+    @pl.when(z>0)
+    def _(): sig(dn)
+    extra=[b for b in range(3,bits)]
+    for b in extra: sig((flip(b),c))
+    pl.semaphore_wait(bar, 3+len(extra)+(z<nz-1).astype(jnp.int32)+(z>0).astype(jnp.int32))
+    dest={'x':xn,'y':yn,'u':up,'d':dn}
+    there={'u':z<nz-1,'d':z>0}
+    opposite={'u':'d','d':'u','x':'x','y':'y'}
+    bufof={'x':0,'y':1,'u':2,'d':2}
+    def rws(i): return ins[pieces[i][0]].shape[0]//(nz*4)
+    def half(i,h):
+        w,c0,cols,order=pieces[i]
+        n=ins[w].shape[1]
+        return pl.ds(pl.multiple_of(h*(n//2)+c0,128),cols)
+    def own_copy(i): return pltpu.make_async_copy(ins[pieces[i][0]].at[:,half(i,c)],own[i],own_sem.at[i])
+    def sib_copy(i): return pltpu.make_async_remote_copy(src_ref=ins[pieces[i][0]].at[:,half(i,1-c)],dst_ref=sibb[i],send_sem=sib_send.at[i],recv_sem=sib_recv.at[i],device_id=sib,device_id_type=MESH)
+    def vcopy(k):
+        dev = sib if k==0 else (flip(k-1),c)
+        return pltpu.make_async_remote_copy(src_ref=vbuf.at[0,k],dst_ref=vbuf.at[1,k],send_sem=vsend.at[k],recv_sem=vrecv.at[k],device_id=dev,device_id_type=MESH)
+    for i in range(npc):
+        sib_copy(i).start(); own_copy(i).start()
+    vbuf[0,0]=vec[...]
+    vcopy(0).start()
+    def blk(i,s): r=rws(i); return pl.ds(pl.multiple_of(s*r,r),r)
+    def message(i,s,pos,d):
+        order=pieces[i][3]
+        b=bufof[d]
+        return pltpu.make_async_remote_copy(src_ref=own[i].at[blk(i,s)],dst_ref=rbuf[i][b].at[slot_index(order,opposite[d],nz,pos)],send_sem=send.at[i,s],recv_sem=recv.at[i,b,slot_index(order,opposite[d],nz,pos)],device_id=dest[d],device_id_type=MESH)
+    def arrival(i,pos,d):
+        order=pieces[i][3]; b=bufof[d]; k=slot_index(order,d,nz,pos)
+        return pltpu.make_async_remote_copy(src_ref=rbuf[i][b].at[k],dst_ref=rbuf[i][b].at[k],send_sem=send.at[i,0],recv_sem=recv.at[i,b,k],device_id=sib,device_id_type=MESH)
+    def add(i,s,pos,children,final):
+        order=pieces[i][3]; r=rws(i)
+        ks=[(bufof[d],slot_index(order,d,nz,pos)) for d in children]
+        @pl.loop(0,r//16)
+        def _(k):
+            rr=pl.ds(pl.multiple_of(k*16,16),16)
+            gr=pl.ds(pl.multiple_of(s*r+k*16,16),16)
+            t=own[i][gr].astype(jnp.float32)+sibb[i][gr].astype(jnp.float32)
+            for b,q in ks: t=t+rbuf[i][b][q,rr].astype(jnp.float32)
+            if final: res[i][rr]=t
+            else: own[i][gr]=t.astype(jnp.bfloat16)
+    def parent(order,bx,by,sgn):
+        differs={'x':bx,'y':by,'z':int(sgn!=0)}
+        last=max(j for j,d in enumerate(order) if differs[d])
+        if order[last]=='z': return 'd' if sgn<0 else 'u'
+        return order[last]
+    def with_children(i,s,pos,children,final):
+        sure=[d for d in children if d in 'xy']; maybe=[d for d in children if d in 'ud']
+        for d in sure: arrival(i,pos,d).wait_recv()
+        for d in maybe: pl.when(there[d])(lambda d=d: arrival(i,pos,d).wait_recv())
+        if not maybe: add(i,s,pos,sure,final)
+        elif len(maybe)==1:
+            pl.when(there[maybe[0]])(lambda: add(i,s,pos,sure+maybe,final))
+            pl.when(jnp.logical_not(there[maybe[0]]))(lambda: add(i,s,pos,sure,final))
+        else:
+            u,d=there['u'],there['d']
+            pl.when(u&d)(lambda: add(i,s,pos,sure+['u','d'],final))
+            pl.when(u&jnp.logical_not(d))(lambda: add(i,s,pos,sure+['u'],final))
+            pl.when(jnp.logical_not(u)&d)(lambda: add(i,s,pos,sure+['d'],final))
+            if nz==1: add(i,s,pos,sure,final)
+    def each(h,i,leaf,action):
+        order=pieces[i][3]
+        for bx,by,sgn in slots():
+            ch=forwards(order,bx,by,sgn)
+            if leaf is not None and (len(ch)==0)!=leaf: continue
+            k=h-bx-by
+            zs=z+sgn*k
+            if sgn==0: valid=k==0
+            else: valid=(k>=1)&(zs>=0)&(zs<nz)
+            pos={'x':x+bx-2*bx*x,'y':y+by-2*by*y,'z':zs}
+            s=zs*4+pos['y']*2+pos['x']
+            pl.when(valid)(lambda s=s,pos=pos,ch=ch,p=parent(order,bx,by,sgn): action(i,s,pos,ch,p))
+    def work(i,s,pos,ch,p):
+        with_children(i,s,pos,ch,False)
+        message(i,s,pos,p).start()
+    def done(i,s,pos,ch,p):
+        message(i,s,pos,p).wait_send()
+    top=nz+1
+    for i in range(npc):
+        own_copy(i).wait(); sib_copy(i).wait_recv()
+        for q in range(LEAD+1): each(jnp.int32(top-q),i,True,work)
+    @pl.loop(0,top)
+    def _(q):
+        h=top-q
+        for i in range(npc):
+            each(h,i,False,work)
+        for i in range(npc):
+            each(h-LEAD-1,i,True,work)
+        for k in range(bits+1):
+            @pl.when(q==k)
+            def _(k=k):
+                vcopy(k).wait()
+                vbuf[0,k+1]=vbuf[0,k]+vbuf[1,k]
+                if k<bits: vcopy(k+1).start()
+    for k in range(top,bits+1):
+        vcopy(k).wait()
+        vbuf[0,k+1]=vbuf[0,k]+vbuf[1,k]
+        if k<bits: vcopy(k+1).start()
+    def out_copy(i): return pltpu.make_async_copy(res[i],outs[pieces[i][0]].at[:,half(i,c)],res_sem.at[i])
+    def out_sib(i,h): return pltpu.make_async_remote_copy(src_ref=res[i],dst_ref=outs[pieces[i][0]].at[:,half(i,h)],send_sem=res_send.at[i],recv_sem=res_recv.at[i],device_id=sib,device_id_type=MESH)
+    for i in range(npc):
+        with_children(i,f,{'x':x,'y':y,'z':z},forwards(pieces[i][3],0,0,0),True)
+        out_sib(i,c).start(); out_copy(i).start()
+    vout[...]=vbuf[0,bits+1]
+    for i in range(npc): sib_copy(i).wait_send()
+    @pl.loop(0,top)
+    def _(q):
+        for i in range(npc): each(top-q,i,None,done)
+    for i in range(npc):
+        out_copy(i).wait(); out_sib(i,c).wait_send(); out_sib(i,1-c).wait_recv()
+
+def reduce_scatter(grads, vec, pieces, nz, cid=2):
+    nw=len(grads); npc=len(pieces); n=nz*4; bits=n.bit_length()-1
+    shards=[(g.shape[0]//n,g.shape[1]) for g in grads]
+    sc=[]
+    B=jnp.bfloat16
+    for w,c0,cols,o in pieces: sc.append(pltpu.VMEM((shards[w][0]*n,cols),B))
+    for w,c0,cols,o in pieces: sc.append(pltpu.VMEM((shards[w][0]*n,cols),B))
+    most=1
+    for w,c0,cols,o in pieces:
+        ns=[slot_count(o,'x',nz),slot_count(o,'y',nz),slot_count(o,'u',nz)]
+        most=max(most,*ns)
+        for k in ns: sc.append(pltpu.VMEM((k,shards[w][0],cols),B))
+    for w,c0,cols,o in pieces: sc.append(pltpu.VMEM((shards[w][0],cols),jnp.float32))
+    D=pltpu.SemaphoreType.DMA
+    sc += [pltpu.VMEM((2,bits+2)+vec.shape,jnp.float32),D((npc,)),D((npc,)),D((npc,)),D((npc,n)),D((npc,3,most)),D((npc,)),D((npc,)),D((npc,)),D((bits+1,)),D((bits+1,))]
+    return pl.pallas_call(functools.partial(rs_kernel,nz,pieces,nw),
+        out_shape=[jax.ShapeDtypeStruct(s,jnp.float32) for s in shards]+[jax.ShapeDtypeStruct(vec.shape,jnp.float32)],
+        in_specs=[pl.BlockSpec(memory_space=pl.ANY)]*nw+[pl.BlockSpec(memory_space=pltpu.VMEM)],
+        out_specs=[pl.BlockSpec(memory_space=pl.ANY)]*nw+[pl.BlockSpec(memory_space=pltpu.VMEM)],
+        scratch_shapes=sc,
+        compiler_params=pltpu.CompilerParams(collective_id=cid,has_side_effects=True,vmem_limit_bytes=58*2**20),
+        name="reduce_gradients")(*grads,vec)
+
+ZXY = ("z", "x", "y")
+ZYX = ("z", "y", "x")
+XYZ = ("x", "y", "z")
+YXZ = ("y", "x", "z")
+ROUTES = (
+    (7, XYZ), (8, YXZ), (0, ZXY), (3, ZYX), (2, ZXY), (1, ZYX), (5, ZYX), (4, ZYX), (6, ZXY),
+)
+
+
+def gather_pieces(shards):
+    pieces = [(w, 0, shards[w].shape[1] // 2, order, True) for w, order in ROUTES]
+    return [(len(shards), 0, 128, ZXY, False)] + pieces
+
+
+def reduce_pieces(shards):
+    return [(w, 0, shards[w].shape[1] // 2, order) for w, order in ROUTES]
+
+
+def whole_tiles(shards):
+    return all(s.shape[0] % 16 == 0 and s.shape[1] % 256 == 0 for s in shards)
+
+
+def gather_all(matrices, vectors, devices):
+    if devices % 4 or not whole_tiles(matrices):
+        def whole(part):
+            return lax.all_gather(part, "fsdp", axis=0, tiled=True)
+        return [whole(m) for m in matrices], [whole(v) for v in vectors]
+    rows = [jnp.pad(v, (0, 128 - v.shape[0])) for v in vectors]
+    packed = jnp.pad(jnp.stack(rows), ((0, 16 - len(rows)), (0, 0)))
+    got = all_gather(list(matrices) + [packed], gather_pieces(matrices), devices // 4)
+    tiles = got[-1].reshape(devices, 16, 128)
+    return got[:-1], [tiles[:, k, : v.shape[0]].reshape(-1) for k, v in enumerate(vectors)]
+
+
+def reduce_all(grads, vectors, devices):
+    if devices % 4 or not whole_tiles([jax.ShapeDtypeStruct((g.shape[0] // devices, g.shape[1]), g.dtype) for g in grads]):
+        def share(part):
+            part = lax.psum(part.astype(jnp.float32), "dp")
+            return lax.psum_scatter(part, "fsdp", scatter_dimension=0, tiled=True)
+        return [share(g) for g in grads], [share(v) for v in vectors]
+    width = max(v.shape[0] for v in vectors)
+    packed = jnp.stack([jnp.pad(v, (0, width - v.shape[0])) for v in vectors])
+    packed = jnp.pad(packed, ((0, 8 - len(vectors)), (0, 0)))
+    got = reduce_scatter(grads, packed, reduce_pieces(grads), devices // 4)
+    me = lax.axis_index("fsdp")
+    shares = []
+    for k, v in enumerate(vectors):
+        n = v.shape[0] // devices
+        shares.append(lax.dynamic_slice(got[-1][k], (me * n,), (n,)))
+    return got[:-1], shares
 
 
 def layer_norm(inputs, scales):
@@ -302,24 +638,14 @@
         window_layout(wide_count, wide_columns, shift_wide),
         window_layout(narrow_count, narrow_columns, narrow_shifts),
     ]
-    enc_full = (
-        lax.all_gather(enc_norm1, "fsdp", axis=0, tiled=True),
-        lax.all_gather(enc_qkv, "fsdp", axis=0, tiled=True),
-        lax.all_gather(enc_out, "fsdp", axis=0, tiled=True),
-        lax.all_gather(enc_norm2, "fsdp", axis=0, tiled=True),
-        lax.all_gather(enc_up, "fsdp", axis=0, tiled=True),
-        lax.all_gather(enc_down, "fsdp", axis=0, tiled=True),
-        lax.all_gather(embed_proj, "fsdp", axis=0, tiled=True),
-    )
-    dec_full = (
-        lax.all_gather(mask_token, "fsdp", axis=0, tiled=True),
-        lax.all_gather(dec_norm1, "fsdp", axis=0, tiled=True),
-        lax.all_gather(dec_qkv, "fsdp", axis=0, tiled=True),
-        lax.all_gather(dec_out, "fsdp", axis=0, tiled=True),
-        lax.all_gather(dec_norm2, "fsdp", axis=0, tiled=True),
-        lax.all_gather(dec_up, "fsdp", axis=0, tiled=True),
-        lax.all_gather(dec_down, "fsdp", axis=0, tiled=True),
-    )
+    devices = lax.axis_size("fsdp")
+    matrices = (
+        enc_qkv, enc_out, enc_up, enc_down, embed_proj, dec_qkv, dec_out, dec_up, dec_down,
+    )
+    vectors = (enc_norm1, enc_norm2, mask_token, dec_norm1, dec_norm2)
+    m, v = gather_all(matrices, vectors, devices)
+    enc_full = (v[0], m[0], m[1], v[1], m[2], m[3], m[4])
+    dec_full = (v[2], v[3], m[5], m[6], v[4], m[7], m[8])
     enc_input = jnp.concatenate(
         [clips_wide.reshape(-1, model_width), clips_narrow.reshape(-1, model_width)], 0
     ).astype(jnp.float32)
@@ -348,15 +674,7 @@
     grad_decoded = jnp.concatenate(
         [cotan_wide.reshape(-1, decoder_width), cotan_narrow.reshape(-1, decoder_width)], 0
     ).astype(jnp.float32)
-    dec_back = (
-        lax.all_gather(dec_norm1, "fsdp", axis=0, tiled=True),
-        lax.all_gather(dec_qkv, "fsdp", axis=0, tiled=True),
-        lax.all_gather(dec_out, "fsdp", axis=0, tiled=True),
-        lax.all_gather(dec_norm2, "fsdp", axis=0, tiled=True),
-        lax.all_gather(dec_up, "fsdp", axis=0, tiled=True),
-        lax.all_gather(dec_down, "fsdp", axis=0, tiled=True),
-    )
-    dec_saved = block_forward(dec_input, dec_back, dec_layouts, DHEADS)[1]
+    dec_back = dec_full[1:]
     grad_canvas, dec_grads = block_backward(grad_decoded, dec_saved, dec_back, dec_layouts, DHEADS)
     wide_patch_rows = wide_count * wide_patches
     grad_canvas_wide = grad_canvas[:wide_patch_rows].reshape(
@@ -375,81 +693,21 @@
         ],
         0,
     ).astype(jnp.bfloat16)
-    enc_back = (
-        lax.all_gather(enc_norm1, "fsdp", axis=0, tiled=True),
-        lax.all_gather(enc_qkv, "fsdp", axis=0, tiled=True),
-        lax.all_gather(enc_out, "fsdp", axis=0, tiled=True),
-        lax.all_gather(enc_norm2, "fsdp", axis=0, tiled=True),
-        lax.all_gather(enc_up, "fsdp", axis=0, tiled=True),
-        lax.all_gather(enc_down, "fsdp", axis=0, tiled=True),
-        lax.all_gather(embed_proj, "fsdp", axis=0, tiled=True),
-    )
+    enc_back = enc_full
     grad_proj = matmul_tn(encoded_low, grad_embedded)
     grad_encoded = matmul_nt(grad_embedded, enc_back[6])
     grad_input, enc_grads = block_backward(
         grad_encoded, enc_saved, enc_back[:6], enc_layouts, HEADS
     )
-    all_shares = (
-        lax.psum_scatter(enc_grads[0], ("fsdp", "dp"), scatter_dimension=0, tiled=True),
-        lax.psum_scatter(enc_grads[1], ("fsdp", "dp"), scatter_dimension=0, tiled=True),
-        lax.psum_scatter(enc_grads[2], ("fsdp", "dp"), scatter_dimension=0, tiled=True),
-        lax.psum_scatter(enc_grads[3], ("fsdp", "dp"), scatter_dimension=0, tiled=True),
-        lax.psum_scatter(enc_grads[4], ("fsdp", "dp"), scatter_dimension=0, tiled=True),
-        lax.psum_scatter(enc_grads[5], ("fsdp", "dp"), scatter_dimension=0, tiled=True),
-        lax.psum_scatter(grad_proj, ("fsdp", "dp"), scatter_dimension=0, tiled=True),
-        lax.psum_scatter(grad_filler, ("fsdp", "dp"), scatter_dimension=0, tiled=True),
-        lax.psum_scatter(dec_grads[0], ("fsdp", "dp"), scatter_dimension=0, tiled=True),
-        lax.psum_scatter(dec_grads[1], ("fsdp", "dp"), scatter_dimension=0, tiled=True),
-        lax.psum_scatter(dec_grads[2], ("fsdp", "dp"), scatter_dimension=0, tiled=True),
-        lax.psum_scatter(dec_grads[3], ("fsdp", "dp"), scatter_dimension=0, tiled=True),
-        lax.psum_scatter(dec_grads[4], ("fsdp", "dp"), scatter_dimension=0, tiled=True),
-        lax.psum_scatter(dec_grads[5], ("fsdp", "dp"), scatter_dimension=0, tiled=True),
-    )
-    enc_shares = all_shares[:7]
-    dec_shares = all_shares[7:]
+    low = jnp.bfloat16
+    grads = [
+        enc_grads[1], enc_grads[2], enc_grads[4], enc_grads[5], grad_proj,
+        dec_grads[1], dec_grads[2], dec_grads[4], dec_grads[5],
+    ]
+    gains = [enc_grads[0], enc_grads[3], grad_filler, dec_grads[0], dec_grads[3]]
+    m, v = reduce_all([g.astype(low) for g in grads], gains, devices)
     totals = (
-        lax.all_gather(enc_shares[0].astype(jnp.bfloat16), "dp", axis=0, tiled=True).astype(
-            jnp.float32
-        ),
-        lax.all_gather(enc_shares[1].astype(jnp.bfloat16), "dp", axis=0, tiled=True).astype(
-            jnp.float32
-        ),
-        lax.all_gather(enc_shares[2].astype(jnp.bfloat16), "dp", axis=0, tiled=True).astype(
-            jnp.float32
-        ),
-        lax.all_gather(enc_shares[3].astype(jnp.bfloat16), "dp", axis=0, tiled=True).astype(
-            jnp.float32
-        ),
-        lax.all_gather(enc_shares[4].astype(jnp.bfloat16), "dp", axis=0, tiled=True).astype(
-            jnp.float32
-        ),
-        lax.all_gather(enc_shares[5].astype(jnp.bfloat16), "dp", axis=0, tiled=True).astype(
-            jnp.float32
-        ),
-        lax.all_gather(enc_shares[6].astype(jnp.bfloat16), "dp", axis=0, tiled=True).astype(
-            jnp.float32
-        ),
-        lax.all_gather(dec_shares[0].astype(jnp.bfloat16), "dp", axis=0, tiled=True).astype(
-            jnp.float32
-        ),
-        lax.all_gather(dec_shares[1].astype(jnp.bfloat16), "dp", axis=0, tiled=True).astype(
-            jnp.float32
-        ),
-        lax.all_gather(dec_shares[2].astype(jnp.bfloat16), "dp", axis=0, tiled=True).astype(
-            jnp.float32
-        ),
-        lax.all_gather(dec_shares[3].astype(jnp.bfloat16), "dp", axis=0, tiled=True).astype(
-            jnp.float32
-        ),
-        lax.all_gather(dec_shares[4].astype(jnp.bfloat16), "dp", axis=0, tiled=True).astype(
-            jnp.float32
-        ),
-        lax.all_gather(dec_shares[5].astype(jnp.bfloat16), "dp", axis=0, tiled=True).astype(
-            jnp.float32
-        ),
-        lax.all_gather(dec_shares[6].astype(jnp.bfloat16), "dp", axis=0, tiled=True).astype(
-            jnp.float32
-        ),
+        v[0], m[0], m[1], v[1], m[2], m[3], m[4], v[2], v[3], m[5], m[6], v[4], m[7], m[8],
     )
     encoded_wide = encoded_low[:wide_rows].reshape(wide_count, wide_visible, model_width)
     encoded_narrow = encoded_low[wide_rows:].reshape(narrow_count, narrow_visible, model_width)

time: 1720 us -> 674 us (0.39)
  waiting for transfers between devices: 1020 us -> 0 us
  Pallas kernels: 0 us -> 194 us
  blocking collectives: 182 us -> 0 us
    reduce_scatter x9 -> x0, waiting for transfers between devices: 813 us -> none  [the longest x1 139 us: local(): lax.psum_scatter(enc_grads[1], ('fsdp', 'dp'), scatter_dimension=0, tiled...]
    all_gather x7 -> x0, waiting for transfers between devices: 202 us -> none  [the longest x1 80.9 us: local(): lax.all_gather(enc_up, 'fsdp', axis=0, tiled=True)]
    pallas_call x0 -> x2, Pallas kernels: none -> 194 us  [the longest x1 104 us: reduce_scatter(): pl.pallas_call(functools.partial(rs_kernel, nz, pieces, nw), out_shape=[j...]
    all_gather x11 -> x0, blocking collectives: 113 us -> none  [the longest x1 40.6 us: local(): lax.all_gather(dec_out, 'fsdp', axis=0, tiled=True)]
    unnamed x3 -> x0, blocking collectives: 69.1 us -> none
    convert_element_type x25 -> x0, other arithmetic: 17.2 us -> none  [the longest x1 0.98 us: local(): enc_shares[5].astype(jnp.bfloat16)]
  transfers between devices with their start and end apart: 16 -> 0, of which waited for: 12 -> 0; matrix products, arithmetic and copies ran while one was open for 23% -> 0% of each run, Pallas kernels for 0% -> 0%
where the time goes in v1:
time: 674 us; the launch traced here: 663 us
  local copies, waits for them, and re-layouts  228 us (34%)
  Pallas kernels  194 us (29%)
  matrix products  171 us (25%)
  other arithmetic  61.8 us (9%)
  between operations  8.84 us (1%)
    pallas_call x1, Pallas kernels, reduce_scatter(): pl.pallas_call(functools.partial(rs_kernel, nz, pieces, nw), out_shape=[j...  104 us
    pallas_call x1, Pallas kernels, all_gather(): pl.pallas_call(functools.partial(ag_kernel, nz, pieces, nw), out_shape=[j...  90.4 us
    dot_general x9, matrix products, matmul(): return jnp.dot(former, latter, preferred_element_type=jnp.float32)  53.4 us
    dot_general x9, matrix products, matmul_nt(): lax.dot_general(former, latter, (((1,), (1,)), ((), ())), preferred_eleme...  34.5 us
    concatenate x12, local copies, waits for them, and re-layouts, attend_back(): jnp.concatenate([grad_queries.reshape(flat_shape), grad_keys.reshape(flat...  30.8 us
    dot_general x9, matrix products, matmul_tn(): lax.dot_general(former, latter, (((0,), (0,)), ((), ())), preferred_eleme...  28.5 us
    unnamed x328, local copies, waits for them, and re-layouts  22.1 us
    concatenate x4, other arithmetic, from_roll_one(): portion = jnp.roll(portion, offsets[0], axis=0)  15.1 us

profile of v1, /device:TPU:11, one launch (start us, length us, event | category | flops | bytes accessed | tf_op | source)
XLA Modules:
  0.0 662.9 jit_solution(2058335577148273673)
XLA Ops:
  6.7 90.4 %gather_weights.1 = (bf16[768,2304]{1,0:T(8,128)(2,1)}, bf16[768,768]{1,0:T(8,128)(2,1)}, bf16[768,3072]{1,0:T(8,128)(2,1)}, bf16[3072,768]{1,0:T(8,128)(2,1)}, ...) custom-call(bf16[48,2304]{1,0:T(8,128)(2,1)} %refs_0_.1, ...), custom_call_target="tpu_custom_call" | custom-call | tf_op jit(solution)/shard_map/gather_weights/pallas_call | solution.py:121
  110.7 9.9 %multiply_convert_fusion.7 = (bf16[204,3072]{1,0:T(8,128)(2,1)S(1)}, f32[204,3072]{1,0:T(8,128)}, f32[204,3072]{1,0:T(8,128)}) fusion(bf16[768,3072]{1,0:T(8,128)(2,1)} %get-tuple-element.51, f32[204,768]{1,0:T(8,128)S(1)} %get-tuple-element.243, f32[768]{0:T(1024)S(1)} %reshape.712, f32[204]{0:T(256)S(1)} %fusion.135, f32[204]{0:T(256)S(1)} %broadcast_multiply_fusion.2), kind=kOutput, calls=%fused_computation.77 | convolution fusion | flops 1003954176 | bytes 11616864 | tf_op jit(solution)/shard_map/dot_general | solution.py:363
  129.3 6.5 scatter_fusion
  171.7 4.4 convert_bitcast_fusion.3
  178.0 4.1 reshape_reshape.45
  191.2 4.1 reshape_reshape.47
  201.9 4.9 gather_fusion.2
  245.8 4.3 convert_bitcast_fusion.2
  252.1 4.1 reshape_transpose_reshape_reshape.3
  276.6 23.7 %multiply_convert_fusion = (bf16[1024,2048]{1,0:T(8,128)(2,1)}, f32[1024,2048]{1,0:T(8,128)S(1)}, f32[1024,2048]{1,0:T(8,128)}) fusion(bf16[512,2048]{1,0:T(8,128)(2,1)} %get-tuple-element.56, f32[1024,512]{1,0:T(8,128)} %copy-done.25, f32[512]{0:T(512)S(1)} %reshape.715, f32[1024]{0:T(1024)S(1)} %fusion.128, f32[1024]{0:T(1024)S(1)} %broadcast_multiply_fusion), kind=kOutput, calls=%fused_computation.17 | convolution fusion | flops 2285895680 | bytes 25176064 | tf_op jit(solution)/shard_map/dot_general | solution.py:363
  300.4 8.0 %add_convert_fusion = bf16[1024,2048]{1,0:T(8,128)(2,1)S(1)} fusion(f32[1024,2048]{1,0:T(8,128)S(1)} %get-tuple-element.194, f32[1024,2048]{1,0:T(8,128)} %get-tuple-element.251, bf16[2048,512]{1,0:T(8,128)(2,1)S(1)} %copy-done.151, bf16[512,512]{1,0:T(8,128)(2,1)S(1)} %bitcast.242, bf16[512,512]{1,0:T(8,128)(2,1)S(1)} %bitcast.246), kind=kOutput, calls=%fused_computation.16 | convolution fusion | flops 2178940928 | bytes 24117248 | tf_op jit(solution)/shard_map/dot_general | solution.py:373
  325.0 5.6 multiply_reduce_fusion.1
  335.5 4.4 concatenate.142
  372.6 4.9 multiply_reduce_fusion
  382.4 4.2 concatenate.146
  391.4 4.1 concatenate.147
  401.8 9.9 %maximum_maximum_fusion = bf16[2,128,4,1536]{3,2,1,0:T(4,128)(2,1)S(1)} fusion(bf16[2,64,4,512]{3,2,1,0:T(4,128)(2,1)} %concatenate.148, bf16[2,64,4,512]{3,2,1,0:T(4,128)(2,1)} %concatenate.147, bf16[2,64,4,512]{3,2,1,0:T(4,128)(2,1)} %concatenate.146), kind=kLoop, calls=%fused_computation.65 | loop fusion | flops 18874368 | bytes 4718592 | tf_op jit(solution)/shard_map/vmap(jit(_roll_dynamic))/concatenate | solution.py:400
  433.5 5.5 multiply_reduce_fusion.5
  442.6 6.1 scatter_fusion.1
  457.3 6.0 add_convert_fusion.1
  463.5 5.2 multiply_reduce_fusion.13
  505.0 6.8 %convolution_convert_fusion.6.refs_7_ = bf16[512,2048]{1,0:T(8,128)(2,1)} fusion(bf16[1024,2048]{1,0:T(8,128)(2,1)} %copy-done.155, f32[1024,512]{1,0:T(8,128)} %copy-done.25, f32[512]{0:T(512)S(1)} %copy-done.141, f32[1024]{0:T(1024)S(1)} %copy-done.123, f32[1024]{0:T(1024)S(1)} %copy-done.111), kind=kOutput, calls=%fused_computation.71 | convolution fusion | flops 2150629376 | bytes 8398848 | tf_op jit(solution)/shard_map/dot_general | solution.py:367
  534.5 103.6 %reduce_gradients.1 = (f32[48,2304]{1,0:T(8,128)}, f32[48,768]{1,0:T(8,128)}, f32[48,3072]{1,0:T(8,128)}, f32[192,768]{1,0:T(8,128)}, f32[48,512]{1,0:T(8,128)},...) custom-call(bf16[768,2304]{1,0:T(8,128)(2,1)} %convolution_convert_f, ...), custom_call_target="tpu_custom_call" | custom-call | tf_op jit(solution)/shard_map/reduce_gradients/pallas_call | solution.py:291
  648.2 5.2 add_convert_fusion.2
  (559 shorter events, 318.4 us)
Async XLA Ops:
  0.7 97.3 %copy-start.45 = (bf16[1,102,768]{2,1,0:T(8,128)(2,1)S(1)}, bf16[1,102,768]{2,1,0:T(8,128)(2,1)}, u32[]{:S(2)}) copy-start(bf16[1,102,768]{2,1,0:T(8,128)(2,1)} %param.38) | copy-start | bytes 470020
  1.7 106.6 %copy-start.34 = (bf16[102,768]{1,0:T(8,128)(2,1)}, bf16[102,768]{1,0:T(8,128)(2,1)S(1)}, u32[]{:S(2)}) copy-start(bf16[102,768]{1,0:T(8,128)(2,1)S(1)} %reshape.555) | copy-start | bytes 470020
  2.8 98.2 %copy-start.117 = (f32[204]{0:T(256)}, f32[204]{0:T(256)S(1)}, u32[]{:S(2)}) copy-start(f32[204]{0:T(256)S(1)} %broadcast_multiply_fusion.3) | copy-start | bytes 2452
  4.0 97.0 %copy-start.128 = (f32[204]{0:T(256)}, f32[204]{0:T(256)S(1)}, u32[]{:S(2)}) copy-start(f32[204]{0:T(256)S(1)} %fusion.86) | copy-start | bytes 2452
  4.0 97.0 %copy-start.134 = (f32[204]{0:T(256)}, f32[204]{0:T(256)S(1)}, u32[]{:S(2)}) copy-start(f32[204]{0:T(256)S(1)} %fusion.134) | copy-start | bytes 2452
  108.2 12.3 %copy-start.74 = (bf16[102,768]{1,0:T(8,128)(2,1)}, bf16[102,768]{1,0:T(8,128)(2,1)S(1)}, u32[]{:S(2)}) copy-start(bf16[102,768]{1,0:T(8,128)(2,1)S(1)} %reshape_reshape.43) | copy-start | bytes 470020
  109.8 10.8 %copy-start.28 = (f32[204,768]{1,0:T(8,128)}, f32[204,768]{1,0:T(8,128)S(1)}, u32[]{:S(2)}) copy-start(f32[204,768]{1,0:T(8,128)S(1)} %get-tuple-element.243) | copy-start | bytes 1880068
  109.8 10.8 %copy-start.114 = (f32[204]{0:T(256)}, f32[204]{0:T(256)S(1)}, u32[]{:S(2)}) copy-start(f32[204]{0:T(256)S(1)} %broadcast_multiply_fusion.2) | copy-start | bytes 2452
  110.6 9.9 %copy-start.124 = (f32[204]{0:T(256)}, f32[204]{0:T(256)S(1)}, u32[]{:S(2)}) copy-start(f32[204]{0:T(256)S(1)} %fusion.135) | copy-start | bytes 2452
  110.7 9.9 %copy-start.92 = (f32[768]{0:T(1024)}, f32[768]{0:T(1024)S(1)}, u32[]{:S(2)}) copy-start(f32[768]{0:T(1024)S(1)} %reshape.712) | copy-start | bytes 9220
  274.8 37.0 %copy-start.110 = (f32[1024]{0:T(1024)}, f32[1024]{0:T(1024)S(1)}, u32[]{:S(2)}) copy-start(f32[1024]{0:T(1024)S(1)} %broadcast_multiply_fusion) | copy-start | bytes 12292
  276.5 35.2 %copy-start.122 = (f32[1024]{0:T(1024)}, f32[1024]{0:T(1024)S(1)}, u32[]{:S(2)}) copy-start(f32[1024]{0:T(1024)S(1)} %fusion.128) | copy-start | bytes 12292
  276.6 35.1 %copy-start.140 = (f32[512]{0:T(512)}, f32[512]{0:T(512)S(1)}, u32[]{:S(2)}) copy-start(f32[512]{0:T(512)S(1)} %reshape.715) | copy-start | bytes 6148
  276.6 23.7 %copy-start.50 = (bf16[2,256,512]{2,1,0:T(8,128)(2,1)S(1)}, bf16[2,256,512]{2,1,0:T(8,128)(2,1)}, u32[]{:S(2)}) copy-start(bf16[2,256,512]{2,1,0:T(8,128)(2,1)} %param.59) | copy-start | bytes 1572868
  276.6 23.7 %copy-start.53 = (bf16[1,512,512]{2,1,0:T(8,128)(2,1)S(1)}, bf16[1,512,512]{2,1,0:T(8,128)(2,1)}, u32[]{:S(2)}) copy-start(bf16[1,512,512]{2,1,0:T(8,128)(2,1)} %param.58) | copy-start | bytes 1572868
  276.6 23.7 %copy-start.151 = (bf16[2048,512]{1,0:T(8,128)(2,1)S(1)}, bf16[2048,512]{1,0:T(8,128)(2,1)}, u32[]{:S(2)}) copy-start(bf16[2048,512]{1,0:T(8,128)(2,1)} %get-tuple-element.57) | copy-start | bytes 6291460
  454.0 9.4 %copy-start.70 = (bf16[102,512]{1,0:T(8,128)(2,1)}, bf16[102,512]{1,0:T(8,128)(2,1)S(1)}, u32[]{:S(2)}) copy-start(bf16[102,512]{1,0:T(8,128)(2,1)S(1)} %gather_fusion) | copy-start | bytes 313348
  457.3 11.7 %copy-start.31 = (f32[204,768]{1,0:T(8,128)}, f32[204,768]{1,0:T(8,128)S(1)}, u32[]{:S(2)}) copy-start(f32[204,768]{1,0:T(8,128)S(1)} %fusion.121) | copy-start | bytes 1880068
  474.5 12.3 %copy-start.96 = (f32[2,12,51]{2,1,0:T(8,128)S(1)}, f32[2,12,51]{2,1,0:T(8,128)}, u32[]{:S(2)}) copy-start(f32[2,12,51]{2,1,0:T(8,128)} %copy-done.95) | copy-start | bytes 14692
  474.5 13.0 %copy-start.17 = (f32[2,12,51,51]{2,3,1,0:T(8,128)S(1)}, f32[2,12,51,51]{2,3,1,0:T(8,128)}, u32[]{:S(2)}) copy-start(f32[2,12,51,51]{2,3,1,0:T(8,128)} %copy-done.16) | copy-start | bytes 749092
  503.0 8.9 %copy-start.47 = (f32[204,768]{1,0:T(8,128)}, f32[204,768]{1,0:T(8,128)S(1)}, u32[]{:S(2)}) copy-start(f32[204,768]{1,0:T(8,128)S(1)} %get-tuple-element.264) | copy-start | bytes 1880068
  534.5 107.5 %copy-start.143 = (f32[204]{0:T(256)S(1)}, f32[204]{0:T(256)}, u32[]{:S(2)}) copy-start(f32[204]{0:T(256)} %get-tuple-element.181) | copy-start | bytes 2452
  534.5 107.5 %copy-start.133 = (f32[204]{0:T(256)S(1)}, f32[204]{0:T(256)}, u32[]{:S(2)}) copy-start(f32[204]{0:T(256)} %copy-done.132) | copy-start | bytes 2452
  534.5 107.5 %copy-start.136 = (f32[204]{0:T(256)S(1)}, f32[204]{0:T(256)}, u32[]{:S(2)}) copy-start(f32[204]{0:T(256)} %copy-done.134) | copy-start | bytes 2452
  (133 other events, 521.6 us)

commit v2 on v1

v2 whole, which is shorter than its diff:
```python
import functools

import jax
import jax.numpy as jnp
from jax import lax
from jax.experimental import pallas as pl
from jax.experimental.pallas import tpu as pltpu
from jax.sharding import PartitionSpec as P

MESH = pl.DeviceIdType.MESH


def slots():
    out=[]
    for bx in (0,1):
        for by in (0,1):
            for sgn in (0,1,-1):
                if (bx,by,sgn)!=(0,0,0): out.append((bx,by,sgn))
    return out

def forwards(order,bx,by,sgn):
    differs={'x':bx,'y':by,'z':int(sgn!=0)}
    last=max([j for j,d in enumerate(order) if differs[d]],default=-1)
    dirs=[]
    for j,d in enumerate(order):
        if j>last:
            dirs += ['u','d'] if d=='z' else [d]
    if last>=0 and order[last]=='z':
        dirs.append('u' if sgn<0 else 'd')
    return dirs

def ag_kernel(nz, pieces, nw, *refs):
    ins=refs[:nw]; outs=refs[nw:2*nw]
    send, recv, sib_send, sib_recv, loc = refs[2*nw:]
    f=lax.axis_index("fsdp"); c=lax.axis_index("dp")
    z=f//4; y=(f//2)%2; x=f%2
    xn=(f+1-2*x, c); yn=(f+2-4*y, c); up=(f+4,c); dn=(f-4,c); sib=(f,1-c)
    bar=pltpu.get_barrier_semaphore()
    def sig(dev): pl.semaphore_signal(bar,inc=1,device_id=dev,device_id_type=MESH)
    sig(xn); sig(yn); sig(sib)
    @pl.when(z<nz-1)
    def _(): sig(up)
    @pl.when(z>0)
    def _(): sig(dn)
    pl.semaphore_wait(bar, 3+(z<nz-1).astype(jnp.int32)+(z>0).astype(jnp.int32))
    dest={'x':xn,'y':yn,'u':up,'d':dn}
    ok={'x':None,'y':None,'u':z<nz-1,'d':z>0}
    code={'x':0,'y':1,'u':2,'d':3}
    def rows(w): return ins[w].shape[0]
    def region(i, s, half):
        w,c0,cols,order,share=pieces[i]
        r=rows(w)
        n=ins[w].shape[1]
        col=c0 if not share else pl.multiple_of(half*(n//2)+c0,128)
        return outs[w].at[pl.ds(pl.multiple_of(s*r,r),r), pl.ds(col,cols)]
    def own(i):
        w,c0,cols,order,share=pieces[i]
        n=ins[w].shape[1]
        col=c0 if not share else pl.multiple_of(c*(n//2)+c0,128)
        return ins[w].at[:, pl.ds(col,cols)]
    def remote(i,s,src,d):
        return pltpu.make_async_remote_copy(src_ref=src,dst_ref=region(i,s,c),send_sem=send.at[i,s,code[d]],recv_sem=recv.at[i,s],device_id=dest[d],device_id_type=MESH)
    def sibling(i,s):
        return pltpu.make_async_remote_copy(src_ref=region(i,s,c),dst_ref=region(i,s,c),send_sem=sib_send.at[i,s],recv_sem=sib_recv.at[i,s],device_id=sib,device_id_type=MESH)
    def go(i,s,src,dirs):
        for d in dirs:
            if ok[d] is None: remote(i,s,src,d).start()
            else:
                pl.when(ok[d])(lambda d=d: remote(i,s,src,d).start())
    def wait_sends(i,s,src,dirs):
        for d in dirs:
            if ok[d] is None: remote(i,s,src,d).wait_send()
            else:
                pl.when(ok[d])(lambda d=d: remote(i,s,src,d).wait_send())
    locals_=[]
    for i in range(len(pieces)):
        go(i,f,own(i),forwards(pieces[i][3],0,0,0))
    for w in range(nw):
        r=rows(w)
        cp=pltpu.make_async_copy(ins[w],outs[w].at[pl.ds(pl.multiple_of(f*r,r),r)],loc.at[w]); cp.start(); locals_.append(cp)
    def each(h, i, action):
        for bx,by,sgn in slots():
            k=h-bx-by
            zs=z+sgn*k
            if sgn==0: valid=k==0
            else: valid=(k>=1)&(zs>=0)&(zs<nz)
            s=zs*4+(y+by-2*by*y)*2+(x+bx-2*bx*x)
            pl.when(valid)(lambda s=s,bx=bx,by=by,sgn=sgn: action(i,s,forwards(pieces[i][3],bx,by,sgn)))
    def step(i,s,dirs):
        remote(i,s,region(i,s,c),'x').wait_recv()
        go(i,s,region(i,s,c),dirs)
        if pieces[i][4]: sibling(i,s).start()
    def fin(i,s,dirs):
        wait_sends(i,s,region(i,s,c),dirs)
        if pieces[i][4]:
            sibling(i,s).wait_send()
            pltpu.make_async_remote_copy(src_ref=region(i,s,1-c),dst_ref=region(i,s,1-c),send_sem=sib_send.at[i,s],recv_sem=sib_recv.at[i,s],device_id=sib,device_id_type=MESH).wait_recv()
    @pl.loop(1,nz+2)
    def _(h):
        for i in range(len(pieces)):
            each(h,i,step)
    for i in range(len(pieces)):
        wait_sends(i,f,own(i),forwards(pieces[i][3],0,0,0))
    for cp in locals_: cp.wait()
    @pl.loop(1,nz+2)
    def _(h):
        for i in range(len(pieces)):
            each(h,i,fin)

def all_gather(shards, pieces, nz, cid=1):
    nw=len(shards); npc=len(pieces); n=nz*4
    return pl.pallas_call(functools.partial(ag_kernel,nz,pieces,nw),
        out_shape=[jax.ShapeDtypeStruct((s.shape[0]*n,s.shape[1]),s.dtype) for s in shards],
        in_specs=[pl.BlockSpec(memory_space=pl.ANY)]*nw,
        out_specs=[pl.BlockSpec(memory_space=pl.ANY)]*nw,
        scratch_shapes=[pltpu.SemaphoreType.DMA((npc,n,4)),pltpu.SemaphoreType.DMA((npc,n)),pltpu.SemaphoreType.DMA((npc,n)),pltpu.SemaphoreType.DMA((npc,n)),pltpu.SemaphoreType.DMA((nw,))],
        compiler_params=pltpu.CompilerParams(collective_id=cid,has_side_effects=True),
        name="gather_weights")(*shards)

def slot_count(order, d, nz):
    size={'x':2,'y':2,'z':nz}
    j=order.index('z' if d in 'ud' else d)
    k=1
    for e in order[:j]: k*=size[e]
    return k*(nz+1) if d in 'ud' else k

def slot_index(order, d, nz, pos):
    size={'x':2,'y':2,'z':nz}
    j=order.index('z' if d in 'ud' else d)
    k=0
    for e in order[:j]: k=k*size[e]+pos[e]
    if d in 'ud': k=k*(nz+1)+pos['z']+(1 if d=='d' else 0)
    return k

LEAD = 0
def rs_kernel(nz, pieces, nw, *refs):
    ins=refs[:nw]; vec=refs[nw]; outs=refs[nw+1:2*nw+1]; vout=refs[2*nw+1]
    rest=list(refs[2*nw+2:])
    npc=len(pieces)
    own=[rest.pop(0) for _ in range(npc)]
    sibb=[rest.pop(0) for _ in range(npc)]
    rbuf=[[rest.pop(0) for _ in range(3)] for _ in range(npc)]
    res=[rest.pop(0) for _ in range(npc)]
    vbuf, own_sem, sib_send, sib_recv, send, recv, res_sem, res_send, res_recv, vsend, vrecv = rest
    f=lax.axis_index("fsdp"); c=lax.axis_index("dp")
    z=f//4; y=(f//2)%2; x=f%2
    bits=(nz*4).bit_length()-1
    def flip(b): return f+(1<<b)*(1-2*((f//(1<<b))%2))
    xn=(flip(0), c); yn=(flip(1), c); up=(f+4,c); dn=(f-4,c); sib=(f,1-c)
    bar=pltpu.get_barrier_semaphore()
    def sig(dev): pl.semaphore_signal(bar,inc=1,device_id=dev,device_id_type=MESH)
    sig(xn); sig(yn); sig(sib)
    @pl.when(z<nz-1)
    def _(): sig(up)
    @pl.when(z>0)
    def _(): sig(dn)
    extra=[b for b in range(3,bits)]
    for b in extra: sig((flip(b),c))
    pl.semaphore_wait(bar, 3+len(extra)+(z<nz-1).astype(jnp.int32)+(z>0).astype(jnp.int32))
    dest={'x':xn,'y':yn,'u':up,'d':dn}
    there={'u':z<nz-1,'d':z>0}
    opposite={'u':'d','d':'u','x':'x','y':'y'}
    bufof={'x':0,'y':1,'u':2,'d':2}
    def rws(i): return ins[pieces[i][0]].shape[0]//(nz*4)
    def half(i,h):
        w,c0,cols,order=pieces[i]
        n=ins[w].shape[1]
        return pl.ds(pl.multiple_of(h*(n//2)+c0,128),cols)
    def own_copy(i): return pltpu.make_async_copy(ins[pieces[i][0]].at[:,half(i,c)],own[i],own_sem.at[i])
    def sib_copy(i): return pltpu.make_async_remote_copy(src_ref=ins[pieces[i][0]].at[:,half(i,1-c)],dst_ref=sibb[i],send_sem=sib_send.at[i],recv_sem=sib_recv.at[i],device_id=sib,device_id_type=MESH)
    def vcopy(k):
        dev = sib if k==0 else (flip(k-1),c)
        return pltpu.make_async_remote_copy(src_ref=vbuf.at[0,k],dst_ref=vbuf.at[1,k],send_sem=vsend.at[k],recv_sem=vrecv.at[k],device_id=dev,device_id_type=MESH)
    for i in range(npc):
        sib_copy(i).start(); own_copy(i).start()
    vbuf[0,0]=vec[...]
    vcopy(0).start()
    def blk(i,s): r=rws(i); return pl.ds(pl.multiple_of(s*r,r),r)
    def message(i,s,pos,d):
        order=pieces[i][3]
        b=bufof[d]
        return pltpu.make_async_remote_copy(src_ref=own[i].at[blk(i,s)],dst_ref=rbuf[i][b].at[slot_index(order,opposite[d],nz,pos)],send_sem=send.at[i,s],recv_sem=recv.at[i,b,slot_index(order,opposite[d],nz,pos)],device_id=dest[d],device_id_type=MESH)
    def arrival(i,pos,d):
        order=pieces[i][3]; b=bufof[d]; k=slot_index(order,d,nz,pos)
        return pltpu.make_async_remote_copy(src_ref=rbuf[i][b].at[k],dst_ref=rbuf[i][b].at[k],send_sem=send.at[i,0],recv_sem=recv.at[i,b,k],device_id=sib,device_id_type=MESH)
    def add(i,s,pos,children,final):
        order=pieces[i][3]; r=rws(i)
        ks=[(bufof[d],slot_index(order,d,nz,pos)) for d in children]
        @pl.loop(0,r//16)
        def _(k):
            rr=pl.ds(pl.multiple_of(k*16,16),16)
            gr=pl.ds(pl.multiple_of(s*r+k*16,16),16)
            t=own[i][gr].astype(jnp.float32)+sibb[i][gr].astype(jnp.float32)
            for b,q in ks: t=t+rbuf[i][b][q,rr].astype(jnp.float32)
            if final: res[i][rr]=t
            else: own[i][gr]=t.astype(jnp.bfloat16)
    def parent(order,bx,by,sgn):
        differs={'x':bx,'y':by,'z':int(sgn!=0)}
        last=max(j for j,d in enumerate(order) if differs[d])
        if order[last]=='z': return 'd' if sgn<0 else 'u'
        return order[last]
    def with_children(i,s,pos,children,final):
        sure=[d for d in children if d in 'xy']; maybe=[d for d in children if d in 'ud']
        for d in sure: arrival(i,pos,d).wait_recv()
        for d in maybe: pl.when(there[d])(lambda d=d: arrival(i,pos,d).wait_recv())
        if not maybe: add(i,s,pos,sure,final)
        elif len(maybe)==1:
            pl.when(there[maybe[0]])(lambda: add(i,s,pos,sure+maybe,final))
            pl.when(jnp.logical_not(there[maybe[0]]))(lambda: add(i,s,pos,sure,final))
        else:
            u,d=there['u'],there['d']
            pl.when(u&d)(lambda: add(i,s,pos,sure+['u','d'],final))
            pl.when(u&jnp.logical_not(d))(lambda: add(i,s,pos,sure+['u'],final))
            pl.when(jnp.logical_not(u)&d)(lambda: add(i,s,pos,sure+['d'],final))
            if nz==1: add(i,s,pos,sure,final)
    def each(h,i,leaf,action):
        order=pieces[i][3]
        for bx,by,sgn in slots():
            ch=forwards(order,bx,by,sgn)
            if leaf is not None and (len(ch)==0)!=leaf: continue
            k=h-bx-by
            zs=z+sgn*k
            if sgn==0: valid=k==0
            else: valid=(k>=1)&(zs>=0)&(zs<nz)
            pos={'x':x+bx-2*bx*x,'y':y+by-2*by*y,'z':zs}
            s=zs*4+pos['y']*2+pos['x']
            pl.when(valid)(lambda s=s,pos=pos,ch=ch,p=parent(order,bx,by,sgn): action(i,s,pos,ch,p))
    def work(i,s,pos,ch,p):
        with_children(i,s,pos,ch,False)
        message(i,s,pos,p).start()
    def done(i,s,pos,ch,p):
        message(i,s,pos,p).wait_send()
    top=nz+1
    for i in range(npc):
        own_copy(i).wait(); sib_copy(i).wait_recv()
        for q in range(LEAD+1): each(jnp.int32(top-q),i,True,work)
    @pl.loop(0,top)
    def _(q):
        h=top-q
        for i in range(npc):
            each(h,i,False,work)
        for i in range(npc):
            each(h-LEAD-1,i,True,work)
        for k in range(bits+1):
            @pl.when(q==k)
            def _(k=k):
                vcopy(k).wait()
                vbuf[0,k+1]=vbuf[0,k]+vbuf[1,k]
                if k<bits: vcopy(k+1).start()
    for k in range(top,bits+1):
        vcopy(k).wait()
        vbuf[0,k+1]=vbuf[0,k]+vbuf[1,k]
        if k<bits: vcopy(k+1).start()
    def out_copy(i): return pltpu.make_async_copy(res[i],outs[pieces[i][0]].at[:,half(i,c)],res_sem.at[i])
    def out_sib(i,h): return pltpu.make_async_remote_copy(src_ref=res[i],dst_ref=outs[pieces[i][0]].at[:,half(i,h)],send_sem=res_send.at[i],recv_sem=res_recv.at[i],device_id=sib,device_id_type=MESH)
    for i in range(npc):
        with_children(i,f,{'x':x,'y':y,'z':z},forwards(pieces[i][3],0,0,0),True)
        out_sib(i,c).start(); out_copy(i).start()
    vout[...]=vbuf[0,bits+1]
    for i in range(npc): sib_copy(i).wait_send()
    @pl.loop(0,top)
    def _(q):
        for i in range(npc): each(top-q,i,None,done)
    for i in range(npc):
        out_copy(i).wait(); out_sib(i,c).wait_send(); out_sib(i,1-c).wait_recv()

def reduce_scatter(grads, vec, pieces, nz, cid=2):
    nw=len(grads); npc=len(pieces); n=nz*4; bits=n.bit_length()-1
    shards=[(g.shape[0]//n,g.shape[1]) for g in grads]
    sc=[]
    B=jnp.bfloat16
    for w,c0,cols,o in pieces: sc.append(pltpu.VMEM((shards[w][0]*n,cols),B))
    for w,c0,cols,o in pieces: sc.append(pltpu.VMEM((shards[w][0]*n,cols),B))
    most=1
    for w,c0,cols,o in pieces:
        ns=[slot_count(o,'x',nz),slot_count(o,'y',nz),slot_count(o,'u',nz)]
        most=max(most,*ns)
        for k in ns: sc.append(pltpu.VMEM((k,shards[w][0],cols),B))
    for w,c0,cols,o in pieces: sc.append(pltpu.VMEM((shards[w][0],cols),jnp.float32))
    D=pltpu.SemaphoreType.DMA
    sc += [pltpu.VMEM((2,bits+2)+vec.shape,jnp.float32),D((npc,)),D((npc,)),D((npc,)),D((npc,n)),D((npc,3,most)),D((npc,)),D((npc,)),D((npc,)),D((bits+1,)),D((bits+1,))]
    return pl.pallas_call(functools.partial(rs_kernel,nz,pieces,nw),
        out_shape=[jax.ShapeDtypeStruct(s,jnp.float32) for s in shards]+[jax.ShapeDtypeStruct(vec.shape,jnp.float32)],
        in_specs=[pl.BlockSpec(memory_space=pl.ANY)]*nw+[pl.BlockSpec(memory_space=pltpu.VMEM)],
        out_specs=[pl.BlockSpec(memory_space=pl.ANY)]*nw+[pl.BlockSpec(memory_space=pltpu.VMEM)],
        scratch_shapes=sc,
        compiler_params=pltpu.CompilerParams(collective_id=cid,has_side_effects=True,vmem_limit_bytes=58*2**20),
        name="reduce_gradients")(*grads,vec)


TIME = 64
WIN = 4
EPS = 1e-6
F = jnp.float32
B = jnp.bfloat16
VMEM_LIMIT = 60 * 2**20


def dot(a, b):
    return lax.dot_general(a, b, (((1,), (0,)), ((), ())), preferred_element_type=F)


def dot_nt(a, b):
    return lax.dot_general(a, b, (((1,), (1,)), ((), ())), preferred_element_type=F)


def dot_tn(a, b):
    return lax.dot_general(a, b, (((0,), (0,)), ((), ())), preferred_element_type=F)


def iota(shape, dim):
    return lax.broadcasted_iota(jnp.int32, shape, dim)


def norm_stats(x):
    center = jnp.mean(x, axis=-1, keepdims=True)
    shifted = x - center
    spread = jnp.mean(shifted * shifted, axis=-1, keepdims=True)
    scale = lax.rsqrt(spread + EPS)
    return shifted * scale, scale


def norm_back(x, gain, grad):
    unit, scale = norm_stats(x)
    by_gain = grad * unit
    by_unit = grad * gain
    mean_one = jnp.mean(by_unit, axis=-1, keepdims=True)
    mean_two = jnp.mean(by_unit * unit, axis=-1, keepdims=True)
    by_input = scale * (by_unit - mean_one - unit * mean_two)
    return by_input, jnp.sum(by_gain.reshape(-1, 8, x.shape[1]), axis=0)


def gelu_both(u):
    t = 1.0 / (1.0 + (0.3275911 * 0.7071067811865476) * jnp.abs(u))
    bell = jnp.exp(-0.5 * u * u)
    poly = t * (0.127414796 + t * (-0.142248368 + t * (0.7107068705 + t * (-0.7265760135 + t * 0.5307027145))))
    tail = poly * bell
    phi = jnp.where(u < 0, tail, 1.0 - tail)
    return u * phi, phi + u * (bell * 0.3989422804014327)


def spread_vector(tiles, lane, size, devices):
    part = size // devices
    pick = (iota((128, size), 1) % part == iota((128, size), 0)).astype(B)
    wide = dot(tiles, pick)
    rows = iota((tiles.shape[0], size), 0)
    keep = rows == (iota((tiles.shape[0], size), 1) // part) * 16 + lane
    return jnp.sum(jnp.where(keep, wide, 0.0), axis=0, keepdims=True)


def lane_groups(x, op):
    lanes = iota(x.shape, 1)
    width = x.shape[1]
    for d in (1, 2, 4, 8):
        other = jnp.where((lanes & d) != 0, pltpu.roll(x, d, 1), pltpu.roll(x, width - d, 1))
        x = op(x, other)
    return x


HEAD = 32
AREA = WIN * WIN


def stack8(block, mask):
    return jnp.concatenate([block] * 8, axis=0) * mask


def dec_kernel(wc, nc, devices, shw, shn, vis, tiles, m_ref, cotw, cotn, wq_h, wo_h, wu_h, wd_h,
               outw, outn, dm_ref, gq, go, gu, gd, vec_ref,
               wq, wo, wu, wd, perm, sel, mhi, mlo, dz, r_ref, a_ref, qkv, p_ref, o_ref, x1_ref,
               b_ref, h_ref, du, dx1, do_ref, dqkv, dec, dm_acc, acc, sems):
    D = wo.shape[0]
    wide_rows = cotw.shape[1]
    narrow_rows = cotn.shape[1]
    rows = wc * wide_rows + nc * narrow_rows
    T = 256
    nt = rows // T
    wide_tiles = wc * wide_rows // T
    cps = []
    for k, (src, dst) in enumerate(((wq_h, wq), (wo_h, wo), (wu_h, wu), (wd_h, wd))):
        cp = pltpu.make_async_copy(src, dst, sems.at[k])
        cp.start()
        cps.append(cp)
    gain1 = spread_vector(tiles[...], 3, D, devices)
    gain2 = spread_vector(tiles[...], 4, D, devices)
    filler = spread_vector(tiles[...], 2, D, devices)
    mhi[...] = m_ref[...].astype(B)
    mlo[...] = (m_ref[...] - mhi[...].astype(F)).astype(B)
    dm_acc[...] = jnp.zeros_like(dm_acc)
    acc[...] = jnp.zeros_like(acc)
    clips = [(i * wide_rows, wide_rows, 8, shw[i, 0], shw[i, 1], cotw, i, i) for i in range(wc)]
    clips += [(wc * wide_rows + i * narrow_rows, narrow_rows, 4, shn[i], 0, cotn, i, wc + i) for i in range(nc)]
    for base, n, cols, s, r, cot, i, v in clips:
        for k in range(0, n, T):
            j = iota((T, 1), 0) + k
            w, q = j >> 4, j & 15
            wf = cols // WIN
            t = ((w // wf) * WIN + (q >> 2) + s) & (TIME - 1)
            f = ((w % wf) * WIN + (q & 3) + r) & (cols - 1)
            patch = t * cols + f
            where = pl.ds(base + k, T)
            hot = jnp.where(iota((T, n), 1) == patch, 1.0, 0.0).astype(B)
            perm[where, 0:n] = hot
            sel[where] = jnp.where(vis[v:v + 1, :] == patch, 1.0, 0.0).astype(B)
            dz[where] = dot(hot, cot[i]).astype(B)

    def group_rows(t):
        g = jnp.where(t < wide_tiles, t * T // wide_rows, wc + (t - wide_tiles) // 2)
        return pl.ds(pl.multiple_of(g * 128, 128), 128)

    cps[0].wait()

    @pl.loop(0, nt)
    def _(t):
        rr = pl.ds(pl.multiple_of(t * T, T), T)
        g = group_rows(t)
        s = sel[rr]
        seen = jnp.sum(s.astype(F), axis=1, keepdims=True)
        x = dot(s, mhi[g]) + dot(s, mlo[g]) + (1.0 - seen) * filler
        r_ref[rr] = x
        a = (norm_stats(x)[0] * gain1).astype(B)
        a_ref[rr] = a
        qkv[rr] = dot(a, wq[...]).astype(B)

    mask = (iota((128, 256), 0) // AREA == iota((128, 256), 1) // HEAD).astype(B)
    scale = HEAD ** -0.5
    nw = 8

    @pl.loop(0, rows // (nw * AREA))
    def _(g):
        base = pl.multiple_of(g * nw * AREA, nw * AREA)
        rr = pl.ds(base, nw * AREA)
        for a in range(D // 256):
            cq = pl.ds(a * 256, 256)
            q, k, v = qkv[rr, cq], qkv[rr, pl.ds(D + a * 256, 256)], qkv[rr, pl.ds(2 * D + a * 256, 256)]
            w16 = [slice(AREA * j, AREA * j + AREA) for j in range(nw)]
            s = jnp.concatenate([dot_nt(q[w], stack8(k[w], mask)) for w in w16], axis=0) * scale
            e = jnp.exp(s - lane_groups(s, jnp.maximum))
            p = e / lane_groups(e, jnp.add)
            p_ref[rr, pl.ds(a * 128, 128)] = p
            low = p.astype(B)
            o_ref[rr, cq] = jnp.concatenate([dot(low[w], stack8(v[w], mask)) for w in w16], axis=0).astype(B)

    for cp in cps[1:]:
        cp.wait()

    @pl.loop(0, nt)
    def _(t):
        rr = pl.ds(pl.multiple_of(t * T, T), T)
        x1 = r_ref[rr] + dot(o_ref[rr], wo[...])
        x1_ref[rr] = x1
        b = (norm_stats(x1)[0] * gain2).astype(B)
        b_ref[rr] = b
        z = dz[rr]
        out = x1
        back = jnp.zeros((T, D), F)
        C = 512
        for k in range(0, wu.shape[1], C):
            u = dot(b, wu[:, k:k + C])
            h, slope = gelu_both(u)
            h = h.astype(B)
            h_ref[rr, k:k + C] = h
            out = out + dot(h, wd[k:k + C, :])
            d = (slope * dot_nt(z, wd[k:k + C, :])).astype(B)
            du[rr, k:k + C] = d
            back = back + dot_nt(d, wu[:, k:k + C])
        dec[rr] = out.astype(B)
        by_input, by_gain = norm_back(x1, gain2, back)
        acc[1] += by_gain
        dx = z.astype(F) + by_input
        dx1[rr] = dx
        do_ref[rr] = dot_nt(dx.astype(B), wo[...]).astype(B)

    for base, n, cols, s, r, cot, i, v in clips:
        res = dot_tn(perm[base:base + n, 0:n], dec[base:base + n]).astype(B)
        if cols == 8:
            outw[i] = res
        else:
            outn[i] = res

    @pl.loop(0, rows // (nw * AREA))
    def _(g):
        base = pl.multiple_of(g * nw * AREA, nw * AREA)
        rr = pl.ds(base, nw * AREA)
        w16 = [slice(AREA * j, AREA * j + AREA) for j in range(nw)]
        for a in range(D // 256):
            cq = pl.ds(a * 256, 256)
            q, k, v = qkv[rr, cq], qkv[rr, pl.ds(D + a * 256, 256)], qkv[rr, pl.ds(2 * D + a * 256, 256)]
            go_ = do_ref[rr, cq]
            ks = [stack8(k[w], mask) for w in w16]
            qs = [stack8(q[w], mask) for w in w16]
            gs = [stack8(go_[w], mask) for w in w16]
            p = p_ref[rr, pl.ds(a * 128, 128)]
            dp = jnp.concatenate([dot_nt(go_[w], stack8(v[w], mask)) for w in w16], axis=0)
            ds = (p * (dp - lane_groups(dp * p, jnp.add))).astype(B)
            dqkv[rr, cq] = (jnp.concatenate([dot(ds[w], m) for w, m in zip(w16, ks)], axis=0) * scale).astype(B)
            s = jnp.concatenate([dot_nt(k[w], m) for w, m in zip(w16, qs)], axis=0) * scale
            s = s.reshape(nw, AREA, 128)
            e = jnp.exp(s - jnp.max(s, axis=1, keepdims=True))
            p = e / jnp.sum(e, axis=1, keepdims=True)
            dp = jnp.concatenate([dot_nt(v[w], m) for w, m in zip(w16, gs)], axis=0).reshape(nw, AREA, 128)
            ds = (p * (dp - jnp.sum(dp * p, axis=1, keepdims=True))).reshape(nw * AREA, 128).astype(B)
            p = p.reshape(nw * AREA, 128).astype(B)
            dqkv[rr, pl.ds(D + a * 256, 256)] = (jnp.concatenate([dot(ds[w], m) for w, m in zip(w16, qs)], axis=0) * scale).astype(B)
            dqkv[rr, pl.ds(2 * D + a * 256, 256)] = jnp.concatenate([dot(p[w], m) for w, m in zip(w16, gs)], axis=0).astype(B)

    @pl.loop(0, nt)
    def _(t):
        rr = pl.ds(pl.multiple_of(t * T, T), T)
        g = group_rows(t)
        by_input, by_gain = norm_back(r_ref[rr], gain1, dot_nt(dqkv[rr], wq[...]))
        acc[0] += by_gain
        dr = dx1[rr] + by_input
        s = sel[rr]
        hidden = 1.0 - jnp.sum(s.astype(F), axis=1, keepdims=True)
        acc[2] += jnp.sum((dr * hidden).reshape(-1, 8, D), axis=0)
        dm_acc[g] += dot_tn(s, dr.astype(B))

    dm_ref[...] = dm_acc[...].astype(B)
    for k in range(3):
        vec_ref[k:k + 1, :] = jnp.sum(acc[k], axis=0, keepdims=True)
    vec_ref[3:, :] = jnp.zeros((5, D), F)
    gd_step = 512

    @pl.loop(0, wd.shape[0] // gd_step)
    def _(k):
        kk = pl.ds(pl.multiple_of(k * gd_step, gd_step), gd_step)
        gd[kk, :] = dot_tn(h_ref[:, kk], dz[...]).astype(B)
        gu[:, kk] = dot_tn(b_ref[...], du[:, kk]).astype(B)

    @pl.loop(0, wq.shape[1] // 512)
    def _(k):
        kk = pl.ds(pl.multiple_of(k * 512, 512), 512)
        gq[:, kk] = dot_tn(a_ref[...], dqkv[:, kk]).astype(B)

    go[...] = dot_tn(o_ref[...], dx1[...].astype(B)).astype(B)


def decoder(m, vis, shw, shn, tiles, cotw, cotn, wq, wo, wu, wd, devices):
    wc, nc = cotw.shape[0], cotn.shape[0]
    D = cotw.shape[2]
    FFD = wu.shape[1]
    rows = wc * cotw.shape[1] + nc * cotn.shape[1]
    V = pl.BlockSpec(memory_space=pltpu.VMEM)
    S = pl.BlockSpec(memory_space=pltpu.SMEM)
    A = pl.BlockSpec(memory_space=pl.ANY)
    sds = jax.ShapeDtypeStruct
    return pl.pallas_call(
        functools.partial(dec_kernel, wc, nc, devices),
        out_shape=[sds(cotw.shape, B), sds(cotn.shape, B), sds(m.shape, B), sds(wq.shape, B), sds(wo.shape, B),
                   sds(wu.shape, B), sds(wd.shape, B), sds((8, D), F)],
        in_specs=[S, S, V, V, V, V, V, A, A, A, A],
        out_specs=[V] * 8,
        scratch_shapes=[
            pltpu.VMEM(wq.shape, B), pltpu.VMEM(wo.shape, B), pltpu.VMEM(wu.shape, B), pltpu.VMEM(wd.shape, B),
            pltpu.VMEM((rows, cotw.shape[1]), B), pltpu.VMEM((rows, 128), B),
            pltpu.VMEM(m.shape, B), pltpu.VMEM(m.shape, B),
            pltpu.VMEM((rows, D), B), pltpu.VMEM((rows, D), F), pltpu.VMEM((rows, D), B), pltpu.VMEM((rows, 3 * D), B),
            pltpu.VMEM((rows, D // 2), F), pltpu.VMEM((rows, D), B), pltpu.VMEM((rows, D), F),
            pltpu.VMEM((rows, D), B), pltpu.VMEM((rows, FFD), B), pltpu.VMEM((rows, FFD), B), pltpu.VMEM((rows, D), F),
            pltpu.VMEM((rows, D), B), pltpu.VMEM((rows, 3 * D), B), pltpu.VMEM((rows, D), B),
            pltpu.VMEM(m.shape, F), pltpu.VMEM((3, 8, D), F), pltpu.SemaphoreType.DMA((4,)),
        ],
        compiler_params=pltpu.CompilerParams(vmem_limit_bytes=VMEM_LIMIT),
        name="decoder_block",
    )(shw, shn, vis, tiles, m, cotw, cotn, wq, wo, wu, wd)


ENC_HEAD = 64


def valid_keys(kind, wide_seen, narrow_seen):
    q, k = iota((128, 128), 0), iota((128, 128), 1)
    if kind == 0:
        return k < wide_seen
    return ((q // 64) == (k // 64)) & (k % 64 < narrow_seen)


def pair_mask():
    return (iota((256, 128), 0) // 128 == iota((256, 128), 1) // ENC_HEAD).astype(B)


def pair_shares(q, k2, valid):
    s2 = dot_nt(q, k2) * (ENC_HEAD ** -0.5)
    shares = []
    for h in range(2):
        s = jnp.where(valid, s2[:, 128 * h:128 * h + 128], -1e30)
        e = jnp.exp(s - jnp.max(s, axis=1, keepdims=True))
        shares.append(e / jnp.sum(e, axis=1, keepdims=True))
    return shares


def load_rows(dst, wide, narrow, wc, nc):
    dst[...] = jnp.zeros_like(dst)
    for i in range(wc):
        dst[128 * i:128 * i + wide.shape[1], :] = wide[i].astype(F)
    for i in range(nc):
        o = 128 * wc + 64 * i
        dst[o:o + narrow.shape[1], :] = narrow[i].astype(F)


def store_rows(src, wide, narrow, wc, nc):
    for i in range(wc):
        wide[i] = src[128 * i:128 * i + wide.shape[1], :]
    for i in range(nc):
        o = 128 * wc + 64 * i
        narrow[i] = src[o:o + narrow.shape[1], :]


def enc_forward_kernel(wc, nc, devices, tiles, cw, cn, wq_h, wo_h, wu_h, wd_h, we_h,
                       encw, encn, m_ref, a_ref, qkv, o_ref, x1_ref, b_ref, h_ref, slope_ref, e_ref,
                       wq, wo, wu, wd, we, x_ref, sems):
    D = wo.shape[0]
    cps = []
    for k, (src, dst) in enumerate(((wq_h, wq), (wo_h, wo), (wu_h, wu), (wd_h, wd), (we_h, we))):
        cp = pltpu.make_async_copy(src, dst, sems.at[k])
        cp.start()
        cps.append(cp)
    load_rows(x_ref, cw, cn, wc, nc)
    gain1 = spread_vector(tiles[...], 0, D, devices)
    gain2 = spread_vector(tiles[...], 1, D, devices)
    x = x_ref[...]
    a = (norm_stats(x)[0] * gain1).astype(B)
    a_ref[...] = a
    cps[0].wait()
    for k in range(0, 3 * D, D):
        qkv[:, k:k + D] = dot(a, wq[:, k:k + D]).astype(B)
    mask = pair_mask()
    groups = x_ref.shape[0] // 128
    for g in range(groups):
        rr = slice(128 * g, 128 * g + 128)
        valid = valid_keys(0 if g < wc else 1, cw.shape[1], cn.shape[1])
        for j in range(D // 128):
            q, k, v = (qkv[rr, o + 128 * j:o + 128 * j + 128] for o in (0, D, 2 * D))
            k2 = jnp.concatenate([k, k], axis=0) * mask
            v2 = jnp.concatenate([v, v], axis=0) * mask
            p2 = jnp.concatenate(pair_shares(q, k2, valid), axis=1).astype(B)
            o_ref[rr, 128 * j:128 * j + 128] = dot(p2, v2).astype(B)
    cps[1].wait()
    x1 = x_ref[...] + dot(o_ref[...], wo[...])
    x1_ref[...] = x1
    b = (norm_stats(x1)[0] * gain2).astype(B)
    b_ref[...] = b
    cps[2].wait()
    cps[3].wait()
    out = x1
    C = 512
    for k in range(0, wu.shape[1], C):
        h, slope = gelu_both(dot(b, wu[:, k:k + C]))
        h = h.astype(B)
        h_ref[:, k:k + C] = h
        slope_ref[:, k:k + C] = slope
        out = out + dot(h, wd[k:k + C, :])
    e_ref[...] = out.astype(B)
    store_rows(e_ref, encw, encn, wc, nc)
    cps[4].wait()
    m_ref[...] = dot(e_ref[...], we[...])


def encoder_forward(tiles, cw, cn, wq, wo, wu, wd, we, devices):
    wc, nc = cw.shape[0], cn.shape[0]
    D = cw.shape[2]
    FFD = wu.shape[1]
    R = 128 * wc + 128 * ((nc + 1) // 2)
    V = pl.BlockSpec(memory_space=pltpu.VMEM)
    A = pl.BlockSpec(memory_space=pl.ANY)
    sds = jax.ShapeDtypeStruct
    return pl.pallas_call(
        functools.partial(enc_forward_kernel, wc, nc, devices),
        out_shape=[sds(cw.shape, B), sds(cn.shape, B), sds((R, we.shape[1]), F), sds((R, D), B), sds((R, 3 * D), B),
                   sds((R, D), B), sds((R, D), F), sds((R, D), B), sds((R, FFD), B), sds((R, FFD), F), sds((R, D), B)],
        in_specs=[V, V, V, A, A, A, A, A],
        out_specs=[V] * 11,
        scratch_shapes=[pltpu.VMEM(w.shape, B) for w in (wq, wo, wu, wd, we)]
        + [pltpu.VMEM((R, D), F), pltpu.SemaphoreType.DMA((5,))],
        compiler_params=pltpu.CompilerParams(vmem_limit_bytes=VMEM_LIMIT),
        name="encoder_forward",
    )(tiles, cw, cn, wq, wo, wu, wd, we)


def enc_backward_kernel(wc, nc, devices, tiles, cw, cn, dm, dec_vec, a_ref, qkv, o_ref, x1_ref, b_ref, h_ref, slope_ref, e_ref,
                        wq_h, wo_h, wu_h, wd_h, we_h,
                        gradw, gradn, gq, go, gu, gd, ge, vec_ref,
                        wq, wo, wu, wd, we, x_ref, do_ref, dqkv, du, sems):
    D = wo.shape[0]
    cps = []
    for k, (src, dst) in enumerate(((we_h, we), (wd_h, wd), (wu_h, wu), (wo_h, wo), (wq_h, wq))):
        cp = pltpu.make_async_copy(src, dst, sems.at[k])
        cp.start()
        cps.append(cp)
    load_rows(x_ref, cw, cn, wc, nc)
    gain1 = spread_vector(tiles[...], 0, D, devices)
    gain2 = spread_vector(tiles[...], 1, D, devices)
    cps[0].wait()
    grad = dot_nt(dm[...], we[...])
    z = grad.astype(B)
    ge[...] = dot_tn(e_ref[...], dm[...]).astype(B)
    cps[1].wait()
    cps[2].wait()
    back = jnp.zeros_like(grad)
    C = 512
    for k in range(0, wu.shape[1], C):
        d = (slope_ref[:, k:k + C] * dot_nt(z, wd[k:k + C, :])).astype(B)
        du[:, k:k + C] = d
        back = back + dot_nt(d, wu[:, k:k + C])
        gd[k:k + C, :] = dot_tn(h_ref[:, k:k + C], z).astype(B)
        gu[:, k:k + C] = dot_tn(b_ref[...], d).astype(B)
    by_input, by_gain = norm_back(x1_ref[...], gain2, back)
    vec_ref[...] = jnp.zeros_like(vec_ref)
    vec_ref[1:2, :] = jnp.sum(by_gain, axis=0, keepdims=True)
    dx1 = grad + by_input
    y = dx1.astype(B)
    cps[3].wait()
    do_ref[...] = dot_nt(y, wo[...]).astype(B)
    go[...] = dot_tn(o_ref[...], y).astype(B)
    mask = pair_mask()
    groups = x_ref.shape[0] // 128
    scale = ENC_HEAD ** -0.5
    lane = iota((128, 128), 1)
    for g in range(groups):
        rr = slice(128 * g, 128 * g + 128)
        valid = valid_keys(0 if g < wc else 1, cw.shape[1], cn.shape[1])
        for j in range(D // 128):
            q, k, v = (qkv[rr, o + 128 * j:o + 128 * j + 128] for o in (0, D, 2 * D))
            g_o = do_ref[rr, 128 * j:128 * j + 128]
            k2 = jnp.concatenate([k, k], axis=0) * mask
            v2 = jnp.concatenate([v, v], axis=0) * mask
            shares = pair_shares(q, k2, valid)
            dp2 = dot_nt(g_o, v2)
            ds, low = [], []
            for h in range(2):
                dp = dp2[:, 128 * h:128 * h + 128]
                p = shares[h]
                ds.append((p * (dp - jnp.sum(dp * p, axis=1, keepdims=True))).astype(B))
                low.append(p.astype(B))
            dq = dot(jnp.concatenate(ds, axis=1), k2) * scale
            dk = jnp.where(lane < ENC_HEAD, dot_tn(ds[0], q), dot_tn(ds[1], q)) * scale
            dv = jnp.where(lane < ENC_HEAD, dot_tn(low[0], g_o), dot_tn(low[1], g_o))
            for o, d in ((0, dq), (D, dk), (2 * D, dv)):
                dqkv[rr, o + 128 * j:o + 128 * j + 128] = d.astype(B)
    cps[4].wait()
    for k in range(0, 3 * D, D):
        gq[:, k:k + D] = dot_tn(a_ref[...], dqkv[:, k:k + D]).astype(B)
    by_input, by_gain = norm_back(x_ref[...], gain1, dot_nt(dqkv[...], wq[...]))
    vec_ref[0:1, :] = jnp.sum(by_gain, axis=0, keepdims=True)
    DD = dec_vec.shape[1]
    vec_ref[2:3, 0:DD] = dec_vec[2:3, :]
    vec_ref[3:5, 0:DD] = dec_vec[0:2, :]
    x_ref[...] = dx1 + by_input
    store_rows(x_ref, gradw, gradn, wc, nc)


def encoder_backward(tiles, cw, cn, dm, dec_vec, saved, wq, wo, wu, wd, we, devices):
    wc, nc = cw.shape[0], cn.shape[0]
    D = cw.shape[2]
    FFD = wu.shape[1]
    R = dm.shape[0]
    V = pl.BlockSpec(memory_space=pltpu.VMEM)
    A = pl.BlockSpec(memory_space=pl.ANY)
    sds = jax.ShapeDtypeStruct
    return pl.pallas_call(
        functools.partial(enc_backward_kernel, wc, nc, devices),
        out_shape=[sds(cw.shape, F), sds(cn.shape, F)] + [sds(w.shape, B) for w in (wq, wo, wu, wd, we)] + [sds((8, D), F)],
        in_specs=[V] * 13 + [A] * 5,
        out_specs=[V] * 8,
        scratch_shapes=[pltpu.VMEM(w.shape, B) for w in (wq, wo, wu, wd, we)]
        + [pltpu.VMEM((R, D), F), pltpu.VMEM((R, D), B), pltpu.VMEM((R, 3 * D), B), pltpu.VMEM((R, FFD), B),
           pltpu.SemaphoreType.DMA((5,))],
        compiler_params=pltpu.CompilerParams(vmem_limit_bytes=VMEM_LIMIT),
        name="encoder_backward",
    )(tiles, cw, cn, dm, dec_vec, *saved, wq, wo, wu, wd, we)


ZXY = ("z", "x", "y")
ZYX = ("z", "y", "x")
XYZ = ("x", "y", "z")
YXZ = ("y", "x", "z")
ROUTES = (
    (7, XYZ), (8, YXZ), (0, ZXY), (3, ZYX), (2, ZXY), (1, ZYX), (5, ZYX), (4, ZYX), (6, ZXY),
)


def whole_tiles(shapes, devices):
    return devices % 4 == 0 and all(r % 16 == 0 and n % 256 == 0 for r, n in shapes)


def gather_all(matrices, vectors, devices):
    rows = [jnp.pad(v, (0, 128 - v.shape[0])) for v in vectors]
    packed = jnp.pad(jnp.stack(rows), ((0, 16 - len(rows)), (0, 0)))
    if not whole_tiles([m.shape for m in matrices], devices):
        got = [lax.all_gather(m, "fsdp", axis=0, tiled=True) for m in (*matrices, packed)]
        return got[:-1], got[-1]
    pieces = [(len(matrices), 0, 128, ZXY, False)]
    pieces += [(w, 0, matrices[w].shape[1] // 2, order, True) for w, order in ROUTES]
    got = all_gather(list(matrices) + [packed], pieces, devices // 4)
    return got[:-1], got[-1]


def reduce_all(grads, packed, sizes, devices):
    if not whole_tiles([(g.shape[0] // devices, g.shape[1]) for g in grads], devices):
        total = lax.psum(packed, ("fsdp", "dp"))
        shares = [
            lax.psum_scatter(lax.psum(g.astype(jnp.float32), "dp"), "fsdp", scatter_dimension=0, tiled=True)
            for g in grads
        ]
    else:
        pieces = [(w, 0, grads[w].shape[1] // 2, order) for w, order in ROUTES]
        *shares, total = reduce_scatter(grads, packed, pieces, devices // 4)
    me = lax.axis_index("fsdp")
    vectors = [lax.dynamic_slice(total[k], (me * (n // devices),), (n // devices,)) for k, n in enumerate(sizes)]
    return shares, vectors


def local(
    clips_wide, clips_narrow, visible_wide, visible_narrow, shift_wide, shift_narrow,
    enc_norm1, enc_qkv, enc_out, enc_norm2, enc_up, enc_down, embed_proj, mask_token,
    dec_norm1, dec_qkv, dec_out, dec_norm2, dec_up, dec_down, cotan_wide, cotan_narrow,
):
    devices = lax.axis_size("fsdp")
    matrices = (enc_qkv, enc_out, enc_up, enc_down, embed_proj, dec_qkv, dec_out, dec_up, dec_down)
    vectors = (enc_norm1, enc_norm2, mask_token, dec_norm1, dec_norm2)
    whole, tiles = gather_all(matrices, vectors, devices)
    enc, dec = whole[:5], whole[5:]
    shown = [jnp.pad(visible_wide, ((0, 0), (0, 128 - visible_wide.shape[1])), constant_values=-1)]
    for i in range(visible_narrow.shape[0]):
        o = 64 * (i % 2)
        shown.append(
            jnp.pad(visible_narrow[i:i + 1], ((0, 0), (o, 128 - o - visible_narrow.shape[1])), constant_values=-1)
        )
    shown = jnp.concatenate(shown, 0)
    encoded_wide, encoded_narrow, embedded, *saved = encoder_forward(tiles, clips_wide, clips_narrow, *enc, devices)
    decoded_wide, decoded_narrow, grad_embedded, *dec_grads, dec_gains = decoder(
        embedded, shown, shift_wide, shift_narrow, tiles, cotan_wide, cotan_narrow, *dec, devices
    )
    grad_wide, grad_narrow, *enc_grads, gains = encoder_backward(
        tiles, clips_wide, clips_narrow, grad_embedded, dec_gains, saved, *enc, devices
    )
    m, v = reduce_all(enc_grads + dec_grads, gains, [n.shape[0] * devices for n in vectors], devices)
    return (
        encoded_wide, encoded_narrow, decoded_wide, decoded_narrow, grad_wide, grad_narrow,
        v[0], m[0], m[1], v[1], m[2], m[3], m[4], v[2], v[3], m[5], m[6], v[4], m[7], m[8],
    )


def solution(mesh):
    clips = ("fsdp", "dp")
    matrix, vector = P("fsdp", None), P("fsdp")
    weights = (
        vector, matrix, matrix, vector, matrix, matrix, matrix, vector,
        vector, matrix, matrix, vector, matrix, matrix,
    )
    rows, pairs = P(clips, None, None), P(clips, None)
    return jax.shard_map(
        local,
        mesh=mesh,
        in_specs=(rows, rows, pairs, pairs, pairs, P(clips), *weights, rows, rows),
        out_specs=(rows,) * 6 + weights,
        check_vma=False,
    )
```

time: 674 us -> 336 us (0.50); the launches traced: 663 us -> 333 us
  local copies, waits for them, and re-layouts: 228 us -> 23.3 us
  matrix products: 171 us -> 0 us
  Pallas kernels: 194 us -> 308 us
  other arithmetic: 61.8 us -> 0.65 us
  between operations: 8.84 us -> 1.03 us
    dot_general x51 -> x0, matrix products: 171 us -> none  [the longest x9 53.4 us: matmul(): return jnp.dot(former, latter, preferred_element_type=jnp.float32)]
    pallas_call x0 -> x3, Pallas kernels: none -> 113 us  [the longest x1 72.7 us: decoder(): pl.pallas_call(functools.partial(dec_kernel, wc, nc, devices), out_shape=...]
    concatenate x23 -> x0, local copies, waits for them, and re-layouts: 44.9 us -> none  [the longest x12 30.8 us: attend_back(): jnp.concatenate([grad_queries.reshape(flat_shape), grad_keys.reshape(flat...]
    gather x14 -> x0, local copies, waits for them, and re-layouts: 37.4 us -> none  [the longest x4 12.4 us: from_roll_one(): return jnp.roll(portion, offsets[1], axis=1)]
    reshape x22 -> x0, local copies, waits for them, and re-layouts: 35.5 us -> none  [the longest x3 8.46 us: attend(): values.reshape(head_shape)]
    another operation x18 -> x0, local copies, waits for them, and re-layouts: 33.3 us -> none  [the longest x3 7.53 us: attend_back(): grad_blended = grad_blended.reshape(head_shape)]
    concatenate x16 -> x1, other arithmetic: 32.4 us -> 0.65 us  [local(): shown = jnp.concatenate(shown, 0)]
    scatter x4 -> x0, local copies, waits for them, and re-layouts: 15.1 us -> none  [the longest x2 7.81 us: place(): return canvas.at[clip_index, visible].set(embedded)]
where the time goes in v2:
time: 336 us; the launch traced here: 333 us
  Pallas kernels  308 us (92%)
  local copies, waits for them, and re-layouts  23.3 us (7%)
    pallas_call x1, Pallas kernels, reduce_scatter(): pl.pallas_call(functools.partial(rs_kernel, nz, pieces, nw), out_shape=[j...  104 us
    pallas_call x1, Pallas kernels, all_gather(): pl.pallas_call(functools.partial(ag_kernel, nz, pieces, nw), out_shape=[j...  90.9 us
    pallas_call x1, Pallas kernels, decoder(): pl.pallas_call(functools.partial(dec_kernel, wc, nc, devices), out_shape=...  72.7 us
    pallas_call x1, Pallas kernels, encoder_backward(): pl.pallas_call(functools.partial(enc_backward_kernel, wc, nc, devices), o...  25.8 us
    unnamed x29, local copies, waits for them, and re-layouts  16.8 us
    pallas_call x1, Pallas kernels, encoder_forward(): pl.pallas_call(functools.partial(enc_forward_kernel, wc, nc, devices), ou...  14.9 us

profile of v2, /device:TPU:11, one launch (start us, length us, event | category | flops | bytes accessed | tf_op | source)
XLA Modules:
  0.0 332.8 jit_solution(8857492320309360749)
XLA Ops:
  0.7 0.7 pad_bitcast_fusion.4
  1.3 0.7 pad_bitcast_fusion.2
  2.0 0.7 pad_bitcast_fusion
  2.7 0.6 pad.38.refs_9_
  3.3 90.9 %gather_weights.1 = (bf16[768,2304]{1,0:T(8,128)(2,1)}, bf16[768,768]{1,0:T(8,128)(2,1)}, bf16[768,3072]{1,0:T(8,128)(2,1)}, bf16[3072,768]{1,0:T(8,128)(2,1)}, ...) custom-call(bf16[48,2304]{1,0:T(8,128)(2,1)} %refs_0_.1, ...), custom_call_target="tpu_custom_call" | custom-call | tf_op jit(solution)/shard_map/gather_weights/pallas_call | solution.py:112
  94.2 1.6 copy.42.cn
  95.8 14.9 %encoder_forward.1 = (bf16[1,102,768]{2,1,0:T(8,128)(2,1)}, bf16[2,51,768]{2,1,0:T(8,128)(2,1)}, f32[256,512]{1,0:T(8,128)}, bf16[256,768]{1,0:T(8,128)(2,1)}, b...) custom-call(bf16[256,128]{1,0:T(8,128)(2,1)} %get-tuple-element.67.t, ...), custom_call_target="tpu_custom_call" | custom-call | tf_op jit(solution)/shard_map/encoder_forward/pallas_call | solution.py:668
  110.7 1.7 copy.44
  112.4 0.7 select_add_fusion.vis
  113.1 72.7 %decoder_block.1 = (bf16[1,512,512]{2,1,0:T(8,128)(2,1)}, bf16[2,256,512]{2,1,0:T(8,128)(2,1)}, bf16[256,512]{1,0:T(8,128)(2,1)}, bf16[512,1536]{1,0:T(8,128)(2,...) custom-call(s32[1,2]{1,0:T(1,128)} %shw.1, s32[2]{0:T(128)} %shn.1, ...), custom_call_target="tpu_custom_call" | custom-call | tf_op jit(solution)/shard_map/decoder_block/pallas_call | solution.py:548
  185.7 25.8 %encoder_backward.1 = (f32[1,102,768]{2,1,0:T(8,128)}, f32[2,51,768]{2,1,0:T(8,128)}, bf16[768,2304]{1,0:T(8,128)(2,1)}, bf16[768,768]{1,0:T(8,128)(2,1)}, bf16[...) custom-call(bf16[256,128]{1,0:T(8,128)(2,1)} %get-tuple-element.67.tiles, ...), custom_call_target="tpu_custom_call" | custom-call | tf_op jit(solution)/shard_map/encoder_backward/pallas_call | solution.py:761
  211.6 2.0 copy.45
  213.6 1.9 copy.46
  215.5 103.5 %reduce_gradients.1 = (f32[48,2304]{1,0:T(8,128)}, f32[48,768]{1,0:T(8,128)}, f32[48,3072]{1,0:T(8,128)}, f32[192,768]{1,0:T(8,128)}, f32[48,512]{1,0:T(8,128)},...) custom-call(bf16[768,2304]{1,0:T(8,128)(2,1)} %get-tuple-element.94., ...), custom_call_target="tpu_custom_call" | custom-call | tf_op jit(solution)/shard_map/reduce_gradients/pallas_call | solution.py:282
  319.0 1.0 fusion.6
  323.0 1.8 copy.56
  324.8 1.6 copy.57
  326.4 1.9 copy.58
  328.4 0.8 copy.59
  329.2 0.6 copy.60
  329.8 0.7 copy.61
  330.5 0.6 copy.62
  331.1 0.7 copy.63
  331.8 0.7 copy.64
  (23 shorter events, 3.0 us)
Async XLA Ops:
  95.8 16.6 %copy-start.6 = (s32[2,51]{1,0:T(2,128)S(1)}, s32[2,51]{1,0:T(2,128)}, u32[]{:S(2)}) copy-start(s32[2,51]{1,0:T(2,128)} %param.25) | copy-start | bytes 1228
  95.8 16.6 %copy-start.7 = (s32[1,102]{1,0:T(1,128)S(1)}, s32[1,102]{1,0:T(1,128)}, u32[]{:S(2)}) copy-start(s32[1,102]{1,0:T(1,128)} %param.24) | copy-start | bytes 1228
  319.0 9.4 %copy-start = (f32[192,768]{1,0:T(8,128)S(1)}, f32[192,768]{1,0:T(8,128)}, u32[]{:S(2)}) copy-start(f32[192,768]{1,0:T(8,128)} %get-tuple-element.176) | copy-start | bytes 1769476
  319.0 10.2 %copy-start.4 = (f32[48,512]{1,0:T(8,128)S(1)}, f32[48,512]{1,0:T(8,128)}, u32[]{:S(2)}) copy-start(f32[48,512]{1,0:T(8,128)} %get-tuple-element.177) | copy-start | bytes 294916
  319.0 10.8 %copy-start.3 = (f32[32,1536]{1,0:T(8,128)S(1)}, f32[32,1536]{1,0:T(8,128)}, u32[]{:S(2)}) copy-start(f32[32,1536]{1,0:T(8,128)} %get-tuple-element.180) | copy-start | bytes 589828
  320.0 10.5 %copy-start.5 = (f32[32,512]{1,0:T(8,128)S(1)}, f32[32,512]{1,0:T(8,128)}, u32[]{:S(2)}) copy-start(f32[32,512]{1,0:T(8,128)} %get-tuple-element.181) | copy-start | bytes 196612
  323.0 8.2 %copy-start.2 = (f32[32,2048]{1,0:T(8,128)S(1)}, f32[32,2048]{1,0:T(8,128)}, u32[]{:S(2)}) copy-start(f32[32,2048]{1,0:T(8,128)} %get-tuple-element.183) | copy-start | bytes 786436
  324.8 7.0 %copy-start.1 = (f32[128,512]{1,0:T(8,128)S(1)}, f32[128,512]{1,0:T(8,128)}, u32[]{:S(2)}) copy-start(f32[128,512]{1,0:T(8,128)} %get-tuple-element.184) | copy-start | bytes 786436
